TPU v7x, 32 devices: a whole 2x2x4 slice. The times are simulated.
32 devices in a mesh: row: 4 (over y, x), col: 8 (over z, core).
Axes of the slice: x: 2, y: 2, z: 4, core: 2. Of those that a mesh axis runs over, the one named last changes fastest.
Arguments:
- fixed_section: bfloat16 [128, 1024], P('row', 'col'), may hold values from -6 to 6
- moving_section: bfloat16 [128, 1024], P('row', 'col'), may hold values from -6 to 6
- field_init: float32 [2, 128, 1024], P(None, 'row', 'col'), may hold values from -48 to 48
- first_weight: float32 [8, 9], replicated, may hold values from -2 to 2
- first_bias: float32 [8], replicated, may hold values from -0.5 to 0.5
- second_weight: float32 [8, 8, 9], replicated, may hold values from -0.75 to 0.75
Outputs:
- field_change: float32 [2, 128, 1024], P(None, 'row', 'col')
All inputs are finite; a program needn't handle non-finite values.
Results may differ from a plain program's by a relative error of at most 0.011.
Values may be sent and summed in bfloat16 or wider, within the bound.
No kernel may reach another device: no remote copies, remote signals or barrier semaphores. Data moves between devices by JAX's collectives and lax.ppermute only.
A program may use at most 64 MiB of HBM per device.

v0:
```python
import jax
import jax.numpy as jnp
from jax import lax
from jax.experimental import pallas as pl
from jax.experimental.pallas import tpu as pltpu
from jax.sharding import PartitionSpec as P

CH = 8
REACH = 16
ITERS = 3
STIFFNESS = 0.01
STEP = 0.5
EPS = 0.01

TR, TC = 32, 128
HALF = 64
SIDE = 3
PITCH = HALF + 2 * SIDE
FROWS = TR + 2 * SIDE
NQ = 22
HALO_M = REACH + 1 + 2 + 2
LANE0 = HALO_M
EROWS = 72
HROWS = 80
HALO_PAD = 24
PADS = (HALO_PAD, 8, 8, 8)
TALL = TR + 2 * HALO_PAD
FE_BLOCKS = 5
ME_BLOCKS = 9


def _levels(span):
    out = []
    while span > 1:
        cut = (span + 1) // 2
        out.append(cut)
        span = cut
    return out


def _groups():
    out = []
    for g in range(NQ // 2):
        first = max((256 * g) // PITCH - SIDE, -2)
        last = min((256 * g + 255) // PITCH - SIDE, TR + 1)
        start = first + 2
        start -= start % 2
        span = last + 18 + REACH - start + 1
        out.append((start, span + 2, span))
    return out


GROUPS = _groups()


def _split(x):
    hi = x.astype(jnp.bfloat16)
    lo = (x - hi.astype(jnp.float32)).astype(jnp.bfloat16)
    return hi, lo


def _roll(x, shift, axis):
    size = x.shape[axis]
    shift = shift % size
    return x if shift == 0 else pltpu.roll(x, shift, axis)


def _pick(x, index):
    dims = lax.GatherDimensionNumbers(
        offset_dims=(), collapsed_slice_dims=(1,), start_index_map=(1,),
        operand_batching_dims=(0,), start_indices_batching_dims=(0,))
    return lax.gather(x, index[..., None], dims, (1, 1), mode=lax.GatherScatterMode.PROMISE_IN_BOUNDS)


def _dot(a, b):
    return jnp.dot(a, b, preferred_element_type=jnp.float32)


def _tall(own, one, two):
    r, n = lax.axis_index("row"), lax.axis_size("row")
    even = lax.rem(r, 2) == 0
    above = jnp.where(r > 0, jnp.where(even, two, one), 0.0)
    below = jnp.where(r < n - 1, jnp.where(even, one, two), 0.0)
    out, at = [], 0
    for x, pad in zip(own, PADS):
        out.append(jnp.concatenate([above[at:at + pad], x, below[at:at + pad]], axis=0))
        at += pad
    return out


def _fetch(pairs, sems):
    copies = [pltpu.make_async_copy(src, dst, sems.at[k]) for k, (src, dst) in enumerate(pairs)]
    for copy in copies:
        copy.start()
    for copy in copies:
        copy.wait()


def _own(own_ref):
    return [own_ref[TR * k:TR * k + TR] for k in range(4)]


def _pack_rows(mv_ref, fx_ref, fd_ref, one_ref, two_ref, own_ref, mv, fx, fd, sems):
    _fetch([(mv_ref, mv), (fx_ref, fx), (fd_ref, fd)], sems)
    even = lax.rem(lax.axis_index("row"), 2) == 0
    at = 0
    for k, x in enumerate([mv[...].astype(jnp.float32), fx[...].astype(jnp.float32), fd[0], fd[1]]):
        pad = PADS[k]
        own_ref[TR * k:TR * k + TR] = x
        first, last = x[:pad], x[TR - pad:]
        one_ref[at:at + pad] = jnp.where(even, last, first)
        two_ref[at:at + pad] = jnp.where(even, first, last)
        at += pad


def _weights(w1_ref, w2_ref, bias_ref, m1_ref, m2_ref, b_ref, w1, w2, flat, sems):
    _fetch([(w1_ref, w1), (w2_ref, w2)], sems)
    lane = lax.broadcasted_iota(jnp.int32, (CH, 128), 1)
    sub = lax.broadcasted_iota(jnp.int32, (CH, 128), 0)
    flat[0] = jnp.zeros((CH, 128), jnp.float32)
    flat[1] = jnp.zeros((CH, 128), jnp.float32)
    flat[0, :, 0:9] = w1[...]
    for c2 in range(CH):
        flat[1, :, 9 * c2:9 * c2 + 9] = w2[:, c2, :]
    b = jnp.zeros((CH, 128), jnp.float32)
    for c in range(CH):
        b = jnp.where(sub == c, bias_ref[c], b)
    b_ref[...] = b
    hi_rows, lo_rows = [], []
    for y in range(8):
        ky = lane % 16 - y - (HALO_PAD - HALO_M)
        v = _pick(flat[0], jnp.clip(3 * ky + lane // 16, 0, 127))
        v = jnp.where((ky >= 0) & (ky <= 2), v, 0.0)
        hi = v.astype(jnp.bfloat16).astype(jnp.float32)
        hi_rows.append(hi)
        lo_rows.append(v - hi)
    m1_ref[...] = jnp.concatenate(hi_rows + lo_rows, axis=0)[:, :48].astype(jnp.bfloat16)
    hi_rows, lo_rows = [], []
    for kx in range(3):
        for y in range(8):
            halves = []
            for half in range(2):
                at = lane + 128 * half
                at = jnp.where(at >= 80, at - 80, at)
                ky = at // 8 - y
                v = _pick(flat[1], jnp.clip(9 * (at % 8) + 3 * ky + kx, 0, 127))
                halves.append(jnp.where((ky >= 0) & (ky <= 2), v, 0.0))
            v = jnp.concatenate(halves, axis=1)
            hi = v.astype(jnp.bfloat16).astype(jnp.float32)
            wide = lax.broadcasted_iota(jnp.int32, (CH, 256), 1)
            hi_rows.append(hi)
            lo_rows.append(jnp.where(wide < 80, v - hi, 0.0))
    m2_ref[...] = jnp.concatenate(hi_rows + lo_rows, axis=0)[:, :160].astype(jnp.bfloat16)


def _pack_cols(own_ref, up_ref, down_ref, one_ref, two_ref):
    even = lax.rem(lax.axis_index("col"), 2) == 0
    tall = _tall(_own(own_ref), up_ref[...], down_ref[...])
    lane = lax.broadcasted_iota(jnp.int32, (8, 128), 1)
    for i in range(TALL // 8):
        first = last = None
        for k in (3, 2, 1, 0):
            if 8 * i < tall[k].shape[0]:
                v = tall[k][8 * i:8 * i + 8]
                a, b = _roll(v, 32 * k, 1), _roll(v, 32 * k + HALO_M, 1)
                first = a if first is None else jnp.where(lane < 32 * k + 32, a, first)
                last = b if last is None else jnp.where(lane < 32 * k + 32, b, last)
        one_ref[8 * i:8 * i + 8] = jnp.where(even, last, first)
        two_ref[8 * i:8 * i + 8] = jnp.where(even, first, last)


def _windows(own, up, down, one, two):
    c, n = lax.axis_index("col"), lax.axis_size("col")
    even = lax.rem(c, 2) == 0
    left = jnp.where(c > 0, jnp.where(even, two, one), 0.0)
    right = jnp.where(c < n - 1, jnp.where(even, one, two), 0.0)
    out = []
    end = HALO_M - HALF + TC
    for k, x in enumerate(_tall(own, up, down)):
        lane = lax.broadcasted_iota(jnp.int32, x.shape, 1)
        r = x.shape[0]
        lw = jnp.where(lane < HALO_M, _roll(left[:r], -32 * k, 1), _roll(x, HALO_M, 1))
        rw = jnp.where(lane < end, _roll(x, HALO_M - HALF, 1), _roll(right[:r], end - 32 * k, 1))
        out.append((lw, rw))
    return out


def _kernel(own_ref, up_ref, down_ref, one_ref, two_ref, w1_ref, bias_ref, w2_ref, out_ref,
            hs, e3, ef, raw, m1, m2, sq, disp, idx, dat):
    row0, col0 = TR * lax.axis_index("row"), TC * lax.axis_index("col")
    rows, cols = TR * lax.axis_size("row"), TC * lax.axis_size("col")
    lane = lax.broadcasted_iota(jnp.int32, (CH, 128), 1)
    col_ok = []
    for h in range(2):
        c = col0 + HALF * h - LANE0 + lane
        col_ok.append((c >= 0) & (c < cols))
    bias = bias_ref[...]
    moving, fixed, field0, field1 = _windows(
        _own(own_ref), up_ref[...], down_ref[...], one_ref[...], two_ref[...])
    field = [field0[0], field0[1], field1[0], field1[1]]

    def field_row(i):
        return jnp.concatenate([x[i + 8 - SIDE:i + 9 - SIDE] for x in field] + [jnp.zeros((4, 128), jnp.float32)], axis=0)

    def keep(y, h):
        r = row0 + y
        ok = jnp.where((r >= 0) & (r < rows), 1, 0)
        return jnp.where(col_ok[h], ok.astype(jnp.float32), 0.0)

    def embed(image, top, blocks, sink):
        shifted = [jnp.concatenate([_roll(image[h], 1 - kx, 1) for h in range(2)], axis=1) for kx in range(3)]
        known = image[0].shape[0]
        for b in range(blocks + 1):
            if 8 * b + 16 > known:
                for k in range(8 * b, 8 * blocks + 2, 2):
                    hs[0, CH * k:CH * k + 16] = jnp.zeros((16, 256), jnp.bfloat16)
                    hs[1, CH * k:CH * k + 16] = jnp.zeros((16, 256), jnp.bfloat16)
                break
            t = _dot(w1_ref[...], jnp.concatenate([x[8 * b:8 * b + 16] for x in shifted], axis=0).astype(jnp.bfloat16))
            pre = t[:64] + t[64:]
            for h in range(2):
                v = jnp.concatenate([
                    jnp.maximum(pre[CH * k:CH * k + CH, 128 * h:128 * h + 128] + bias, 0.0) * keep(top - 1 + 8 * b + k, h)
                    for k in range(8)], axis=0)
                hi, lo = _split(v)
                hs[0, 64 * b:64 * b + 64, 128 * h:128 * h + 128] = hi
                hs[1, 64 * b:64 * b + 64, 128 * h:128 * h + 128] = lo
        for b in range(blocks):
            t = _dot(w2_ref[...], jnp.concatenate([hs[0, 64 * b:64 * b + 80], hs[1, 64 * b:64 * b + 80]], axis=0))
            v = t[:192] + t[192:]
            for h in range(2):
                o = [v[64 * kx:64 * kx + 64, 128 * h:128 * h + 128] for kx in range(3)]
                e = o[1] + _roll(o[0], 1, 1) + _roll(o[2], -1, 1)
                sink(b, h, [e[CH * k:CH * k + CH] * keep(top + 8 * b + k, h) for k in range(8)])

    fixed_rows = [[], []]

    def fixed_sink(b, h, got):
        fixed_rows[h].extend(got)

    embed(fixed, -3, FE_BLOCKS, fixed_sink)
    for h in range(2):
        cur = jnp.zeros((CH, 128), jnp.float32)
        q = 0
        for i in range(36):
            f0 = PITCH * (i + 1)
            at, o = f0 // 128, f0 % 128
            while q < at:
                ef[h, q] = cur
                q += 1
            v = _roll(fixed_rows[h][i + 1], o - (LANE0 - SIDE), 1)
            cur = jnp.where(lane >= o, v, cur)
            if o + PITCH > 128:
                ef[h, q] = cur
                q += 1
                cur = v
        while q < NQ:
            ef[h, q] = cur
            q += 1

    def moving_sink(b, h, got):
        out = []
        for e0 in got:
            left, right = _roll(e0, 1, 1), _roll(e0, -1, 1)
            p1 = 0.5 * (right - left)
            p2 = 0.5 * (right + left) - e0
            out += [e0 + 0.25 * p2, p1, p2]
        hi, lo = _split(jnp.concatenate(out, axis=0))
        e3[h, 192 * b:192 * b + 192, 0:128] = hi
        e3[h, 192 * b:192 * b + 192, 128:256] = lo

    embed(moving, -(REACH + 3), ME_BLOCKS, moving_sink)

    cur = jnp.zeros((8, 128), jnp.float32)
    q = 0
    for i in range(FROWS):
        f0 = PITCH * i
        at, o = f0 // 128, f0 % 128
        v = _roll(field_row(i), o - (LANE0 - SIDE), 1)
        cur = jnp.where(lane >= o, v, cur)
        if o + PITCH > 128:
            raw[at] = cur
            cur = v
            q = at + 1
    while q < NQ:
        raw[q] = cur
        q += 1
    m1[...] = jnp.zeros_like(m1)
    m2[...] = jnp.zeros_like(m2)
    dat[...] = jnp.zeros_like(dat)

    sub = lax.broadcasted_iota(jnp.int32, (8, 128), 0)
    half_at = HALF * (sub % 2)

    def place(q):
        f = lax.broadcasted_iota(jnp.int32, (8, 128), 1) + 128 * q
        y = jnp.floor((f.astype(jnp.float32) + 0.5) * (1.0 / PITCH)).astype(jnp.int32)
        return y - SIDE, f - y * PITCH

    def shifted(x, q, s):
        if s > 0:
            a = _roll(x[q], -s, 1)
            b = _roll(x[min(q + 1, NQ - 1)], -s, 1)
            return jnp.where(lane < 128 - s, a, b)
        a = _roll(x[q], -s, 1)
        b = _roll(x[max(q - 1, 0)], -s, 1)
        return jnp.where(lane >= -s, a, b)

    iota_k = lax.broadcasted_iota(jnp.int32, (128, 256), 0).astype(jnp.float32).astype(jnp.bfloat16)

    def group(g, h):
        start, count, span = GROUPS[g]

        def pair(ref, s):
            return jnp.concatenate([jnp.broadcast_to(ref[2 * g + k, s:s + 1, :], (8, 128)) for k in range(2)], axis=1)

        col = jnp.concatenate([idx[2 * g + k, 2 + h:3 + h, :] for k in range(2)], axis=1).astype(jnp.bfloat16)
        pick = jnp.where(iota_k == jnp.broadcast_to(col, (128, 256)), jnp.bfloat16(1.0), jnp.bfloat16(0.0))
        t = _dot(e3[h, 24 * start:24 * (start + count), :], jnp.concatenate([pick, pick], axis=0))
        base = pair(idx, h) - (start * 1.0)
        conds = []
        for cut in _levels(span):
            c = base >= cut
            conds.append((cut, c))
            base = jnp.where(c, base - cut, base)
        taps = []
        for b in range(3):
            T = [t[24 * k + 8 * b:24 * k + 8 * b + 8] for k in range(count)]
            for cut, c in conds:
                T = [jnp.where(c, T[k + cut], T[k]) if k + cut < len(T) else T[k] for k in range(cut + 2)]
            taps.append(T)
        fr, fc = pair(disp, 4 + h), pair(disp, 6 + h)
        A, B = [], []
        for a in range(3):
            w = fc * taps[2][a]
            v = taps[1][a] + w
            A.append(taps[0][a] + fc * v)
            B.append(v + w)
        da, qa = 0.5 * (A[2] - A[0]), 0.5 * (A[2] + A[0]) - A[1]
        db, qb = 0.5 * (B[2] - B[0]), 0.5 * (B[2] + B[0]) - B[1]
        wa = fr * qa
        va = da + wa
        warped = A[1] + 0.25 * qa + fr * va
        slope_row = va + wa
        slope_col = B[1] + 0.25 * qb + fr * (db + fr * qb)
        fixed = jnp.concatenate([ef[h, 2 * g], ef[h, 2 * g + 1]], axis=1)
        miss = (warped - fixed) * (2.0 / CH)
        for comp, slope in ((0, slope_row), (1, slope_col)):
            total = jnp.sum(miss * slope, axis=0, keepdims=True)
            for k in range(2):
                s = 2 * comp + h
                dat[2 * g + k, s:s + 1, :] = total[:, 128 * k:128 * k + 128]

    def step(t):
        for q in range(NQ):
            y, j = place(q)
            c = col0 + half_at + j - SIDE
            ok = (row0 + y >= 0) & (row0 + y < rows) & (c >= 0) & (c < cols)
            s = jnp.tanh(raw[q] * (1.0 / REACH))
            d = REACH * s
            n = jnp.floor(d + 0.5)
            sq[q] = s
            fr = d - n
            disp[q] = jnp.where(sub < 4, jnp.where(ok, d, 0.0), _roll(fr, 4, 0))
            first = jnp.where(sub < 2, (y + 18).astype(jnp.float32), (j + (LANE0 - SIDE)).astype(jnp.float32))
            idx[q] = jnp.maximum(n + first, 0.0)
        for g in range(NQ // 2 - (t > 0)):
            for h in range(2):
                group(g, h)
        one, two = 1.0 / (1.0 - 0.9 ** (t + 1)), 1.0 / (1.0 - 0.999 ** (t + 1))
        for q in range(NQ):
            around = shifted(disp, q, 1) + shifted(disp, q, -1) + shifted(disp, q, PITCH) + shifted(disp, q, -PITCH)
            s = sq[q]
            grad = (dat[q] + 2.0 * STIFFNESS * (4.0 * REACH * s - around)) * (1.0 - s * s)
            a = 0.9 * m1[q] + 0.1 * grad
            b = 0.999 * m2[q] + 0.001 * grad * grad
            m1[q] = a
            m2[q] = b
            raw[q] = raw[q] - STEP * (a * one) / (jnp.sqrt(b * two) + EPS)

    for t in range(ITERS):
        step(t)

    for y in range(TR):
        f0 = PITCH * (y + SIDE) + SIDE
        at, o = f0 // 128, f0 % 128
        v = raw[at]
        if o + HALF > 128:
            v = jnp.where(lane >= o, v, raw[at + 1])
        v = _roll(v, -o, 1) - _roll(field_row(y + SIDE), -LANE0, 1)
        w = _roll(v, HALF, 1)
        for comp in range(2):
            out_ref[comp, y:y + 1, 0:HALF] = v[2 * comp:2 * comp + 1, 0:HALF]
            out_ref[comp, y:y + 1, HALF:TC] = w[2 * comp + 1:2 * comp + 2, HALF:TC]


def _swaps(n, first):
    return [p for a in range(first, n, 2) for p in ((a, (a + 1) % n), ((a + 1) % n, a))]


def _exchange(pair, axis):
    n = lax.axis_size(axis)
    return [lax.ppermute(x, axis, _swaps(n, k)) for k, x in enumerate(pair)]


def _local(fixed_section, moving_section, field_init, first_weight, first_bias, second_weight):
    vmem = pl.BlockSpec(memory_space=pltpu.VMEM)
    smem = pl.BlockSpec(memory_space=pltpu.SMEM)
    anywhere = pl.BlockSpec(memory_space=pltpu.HBM)
    f32, bf16 = jnp.float32, jnp.bfloat16

    def call(body, name, out, specs, scratch):
        return pl.pallas_call(
            body,
            out_shape=[jax.ShapeDtypeStruct(*x) for x in out],
            in_specs=specs,
            out_specs=[vmem] * len(out),
            scratch_shapes=scratch,
            compiler_params=pltpu.CompilerParams(vmem_limit_bytes=48 * 2 ** 20),
            name=name,
        )

    strip = ((sum(PADS), 128), f32)
    one, two, own = call(_pack_rows, "pack_rows", [strip, strip, ((4 * TR, TC), f32)], [anywhere] * 3, [
        pltpu.VMEM((TR, TC), bf16), pltpu.VMEM((TR, TC), bf16), pltpu.VMEM((2, TR, TC), f32),
        pltpu.SemaphoreType.DMA((3,))])(*[pltpu.with_memory_space_constraint(x, pltpu.HBM) for x in (moving_section, fixed_section, field_init)])
    up, down = _exchange((one, two), "row")
    w1, w2, bias = call(_weights, "weights", [((128, 48), bf16), ((384, 160), bf16), ((CH, 128), f32)],
                        [anywhere, anywhere, smem], [
        pltpu.VMEM((CH, 9), f32), pltpu.VMEM((CH, CH, 9), f32), pltpu.VMEM((2, CH, 128), f32),
        pltpu.SemaphoreType.DMA((2,))])(first_weight, second_weight, first_bias)
    strip = ((TALL, 128), f32)
    one, two = _exchange(call(_pack_cols, "pack_cols", [strip, strip], [vmem] * 3, [])(own, up, down), "col")
    return call(_kernel, "refine", [((2, TR, TC), f32)], [vmem] * 8, [
        pltpu.VMEM((2, HROWS * CH, 256), bf16),
        pltpu.VMEM((2, EROWS * 24, 256), bf16),
        pltpu.VMEM((2, NQ, CH, 128), f32),
        *[pltpu.VMEM((NQ, 8, 128), f32) for _ in range(7)],
    ])(own, up, down, one, two, w1, bias, w2)[0]


def solution(mesh):
    return jax.shard_map(
        _local,
        mesh=mesh,
        in_specs=(P("row", "col"), P("row", "col"), P(None, "row", "col"), P(), P(), P()),
        out_specs=P(None, "row", "col"),
        check_vma=False,
    )
```

profile of v0, /device:TPU:0, one launch (start us, length us, event | category | flops | bytes accessed | tf_op | source)
XLA Modules:
  0.0 25.0 jit_solution(3886976070279853094)
XLA Ops:
  0.0 0.8 %pack_rows.1 = (f32[48,128]{1,0:T(8,128)S(1)}, f32[48,128]{1,0:T(8,128)S(1)}, f32[128,128]{1,0:T(8,128)S(1)}) custom-call(bf16[32,128]{1,0:T(8,128)(2,1)} %mv_ref.1, bf16[32,128]{1,0:T(8,128)(2,1)} %fx_ref.1, f32[2,32,128]{2,1,0:T(8,128)} %fd_ref.1), custom_call_target="tpu_custom_call" | custom-call | tf_op jit(solution)/shard_map/pack_rows/pallas_call | solution.py:424
  0.8 3.0 %collective-permute-start = (f32[48,128]{1,0:T(8,128)S(1)}, f32[48,128]{1,0:T(8,128)S(1)}, u32[]{:S(2)}, u32[]{:S(2)}) collective-permute-start(f32[48,128]{1,0:T(8,128)S(1)} %get-tuple-element.14), channel_id=1, source_target_pairs={{0,8},{8,0},{16,24},{24,16},{1,9},{9,1},{17,25},{25,17},{2,10},{10... | collective-permute-start | bytes 73736 | tf_op jit(solution)/shard_map/ppermute | solution.py:403
  3.8 1.5 %collective-permute-start.1 = (f32[48,128]{1,0:T(8,128)S(1)}, f32[48,128]{1,0:T(8,128)S(1)}, u32[]{:S(2)}, u32[]{:S(2)}) collective-permute-start(f32[48,128]{1,0:T(8,128)S(1)} %get-tuple-element.15), channel_id=1, source_target_pairs={{8,16},{16,8},{24,0},{0,24},{9,17},{17,9},{25,1},{1,25},{10,18},{1... | collective-permute-start | bytes 73736 | tf_op jit(solution)/shard_map/ppermute | solution.py:403
  5.3 0.3 %collective-permute-done.up_ref = f32[48,128]{1,0:T(8,128)S(1)} collective-permute-done((f32[48,128]{1,0:T(8,128)S(1)}, f32[48,128]{1,0:T(8,128)S(1)}, u32[]{:S(2)}, u32[]{:S(2)}) %collective-permute-start) | collective-permute-done | bytes 24608 | tf_op jit(solution)/shard_map/ppermute | solution.py:403
  5.6 2.9 %collective-permute-done.1.down_ref = f32[48,128]{1,0:T(8,128)S(1)} collective-permute-done((f32[48,128]{1,0:T(8,128)S(1)}, f32[48,128]{1,0:T(8,128)S(1)}, u32[]{:S(2)}, u32[]{:S(2)}) %collective-permute-start.1) | collective-permute-done | bytes 24608 | tf_op jit(solution)/shard_map/ppermute | solution.py:403
  8.6 0.0 copy-start
  8.6 0.0 copy-start.1
  8.6 0.1 pack_cols.1
  8.7 0.0 copy-start.2
  8.7 0.1 collective-permute-start.2
  8.8 3.7 %collective-permute-start.3 = (f32[80,128]{1,0:T(8,128)S(1)}, f32[80,128]{1,0:T(8,128)S(1)}, u32[]{:S(2)}, u32[]{:S(2)}) collective-permute-start(f32[80,128]{1,0:T(8,128)S(1)} %get-tuple-element.17), channel_id=1, source_target_pairs={{1,2},{2,1},{3,4},{4,3},{5,6},{6,5},{7,0},{0,7},{9,10},{10,9},{11,... | collective-permute-start | bytes 122888 | tf_op jit(solution)/shard_map/ppermute | solution.py:403
  12.5 0.0 copy-done
  12.5 0.0 copy-done.1
  12.5 0.0 copy-done.2
  12.5 0.9 %weights.1 = (bf16[128,48]{1,0:T(8,128)(2,1)S(1)}, bf16[384,160]{1,0:T(8,128)(2,1)S(1)}, f32[8,128]{1,0:T(8,128)S(1)}) custom-call(f32[8,9]{1,0:T(8,128)S(1)} %copy-done.1, f32[8,8,9]{2,1,0:T(8,128)S(1)} %copy-done, f32[8]{0:T(128)S(1)} %copy-done.2), custom_call_target="tpu_custom_call" | custom-call | tf_op jit(solution)/shard_map/weights/pallas_call | solution.py:428
  13.4 0.0 collective-permute-done.2.one_ref
  13.4 0.9 %collective-permute-done.3.two_ref = f32[80,128]{1,0:T(8,128)S(1)} collective-permute-done((f32[80,128]{1,0:T(8,128)S(1)}, f32[80,128]{1,0:T(8,128)S(1)}, u32[]{:S(2)}, u32[]{:S(2)}) %collective-permute-start.3) | collective-permute-done | bytes 40992 | tf_op jit(solution)/shard_map/ppermute | solution.py:403
  14.3 10.7 %refine.1 = f32[2,32,128]{2,1,0:T(8,128)} custom-call(f32[128,128]{1,0:T(8,128)S(1)} %get-tuple-element.13.own_ref, f32[48,128]{1,0:T(8,128)S(1)} %collective-permute-done.up_ref, f32[48,128]{1,0:T(8,128)S(1)} %collective-permute-done.1.down_ref, f32[80,128]{1,0:T(8,128)S(1)} %collective-permute-done.2.one_ref, ...), custom_call_target="tpu_custom_call" | custom-call | tf_op jit(solution)/shard_map/refine/pallas_call | solution.py:434
Async XLA Ops:
  0.8 4.8 %collective-permute-start = (f32[48,128]{1,0:T(8,128)S(1)}, f32[48,128]{1,0:T(8,128)S(1)}, u32[]{:S(2)}, u32[]{:S(2)}) collective-permute-start(f32[48,128]{1,0:T(8,128)S(1)} %get-tuple-element.14), channel_id=1, source_target_pairs={{0,8},{8,0},{16,24},{24,16},{1,9},{9,1},{17,25},{25,17},{2,10},{10... | collective-permute-start | bytes 73736 | tf_op jit(solution)/shard_map/ppermute | solution.py:403
  3.8 4.7 %collective-permute-start.1 = (f32[48,128]{1,0:T(8,128)S(1)}, f32[48,128]{1,0:T(8,128)S(1)}, u32[]{:S(2)}, u32[]{:S(2)}) collective-permute-start(f32[48,128]{1,0:T(8,128)S(1)} %get-tuple-element.15), channel_id=1, source_target_pairs={{8,16},{16,8},{24,0},{0,24},{9,17},{17,9},{25,1},{1,25},{10,18},{1... | collective-permute-start | bytes 73736 | tf_op jit(solution)/shard_map/ppermute | solution.py:403
  8.6 3.9 %copy-start = (f32[8,8,9]{2,1,0:T(8,128)S(1)}, f32[8,8,9]{2,1,0:T(8,128)}, u32[]{:S(2)}) copy-start(f32[8,8,9]{2,1,0:T(8,128)} %w2_ref.1) | copy-start | bytes 6916
  8.6 3.9 %copy-start.1 = (f32[8,9]{1,0:T(8,128)S(1)}, f32[8,9]{1,0:T(8,128)}, u32[]{:S(2)}) copy-start(f32[8,9]{1,0:T(8,128)} %w1_ref.1) | copy-start | bytes 868
  8.7 3.8 %copy-start.2 = (f32[8]{0:T(128)S(1)}, f32[8]{0:T(128)}, u32[]{:S(2)}) copy-start(f32[8]{0:T(128)} %bias_ref.1) | copy-start | bytes 100
  8.7 4.7 %collective-permute-start.2 = (f32[80,128]{1,0:T(8,128)S(1)}, f32[80,128]{1,0:T(8,128)S(1)}, u32[]{:S(2)}, u32[]{:S(2)}) collective-permute-start(f32[80,128]{1,0:T(8,128)S(1)} %get-tuple-element.16), channel_id=1, source_target_pairs={{0,1},{1,0},{2,3},{3,2},{4,5},{5,4},{6,7},{7,6},{8,9},{9,8},{10,11... | collective-permute-start | bytes 122888 | tf_op jit(solution)/shard_map/ppermute | solution.py:403
  8.8 5.5 %collective-permute-start.3 = (f32[80,128]{1,0:T(8,128)S(1)}, f32[80,128]{1,0:T(8,128)S(1)}, u32[]{:S(2)}, u32[]{:S(2)}) collective-permute-start(f32[80,128]{1,0:T(8,128)S(1)} %get-tuple-element.17), channel_id=1, source_target_pairs={{1,2},{2,1},{3,4},{4,3},{5,6},{6,5},{7,0},{0,7},{9,10},{10,9},{11,... | collective-permute-start | bytes 122888 | tf_op jit(solution)/shard_map/ppermute | solution.py:403
where the time goes:
time: 25.2 us; the launch traced here: 25 us
  Pallas kernels  12.5 us (50%)
  starting transfers between devices  8.27 us (33%)
  waiting for transfers between devices  4.11 us (16%)
    pallas_call x1, Pallas kernels, _local(): call(_kernel, 'refine', [((2, TR, TC), f32)], [vmem] * 8, [pltpu.VMEM((2,...  10.7 us
    ppermute x4, starting transfers between devices, _exchange(): return [lax.ppermute(x, axis, _swaps(n, k)) for k, x in enumerate(pair)]  8.27 us
    ppermute x4, waiting for transfers between devices, _exchange(): return [lax.ppermute(x, axis, _swaps(n, k)) for k, x in enumerate(pair)]  4.11 us
    pallas_call x1, Pallas kernels, _local(): call(_weights, 'weights', [((128, 48), bf16), ((384, 160), bf16), ((CH, 1...  0.89 us
    pallas_call x1, Pallas kernels, _local(): call(_pack_rows, 'pack_rows', [strip, strip, ((4 * TR, TC), f32)], [anywh...  0.83 us
  transfers between devices with their start and end apart: 4, of which 3 were waited for; matrix products, arithmetic and copies ran while one was open for 0% of the time, Pallas kernels for 4%

commit v1 on v0

--- a/solution.py
+++ b/solution.py
@@ -15,18 +15,25 @@
 TR, TC = 32, 128
 HALF = 64
 SIDE = 3
-PITCH = HALF + 2 * SIDE
-FROWS = TR + 2 * SIDE
-NQ = 22
 HALO_M = REACH + 1 + 2 + 2
+HALO_PAD = 24
+PADS = (HALO_PAD, 8, 8, 8)
+TALL = TR + 2 * HALO_PAD
 LANE0 = HALO_M
 EROWS = 72
 HROWS = 80
-HALO_PAD = 24
-PADS = (HALO_PAD, 8, 8, 8)
-TALL = TR + 2 * HALO_PAD
 FE_BLOCKS = 5
 ME_BLOCKS = 9
+
+SEGS = 5
+WIDE = 26
+NQ = 10
+CUT = 20
+PROWS = EROWS - CUT
+
+
+def _segment(s):
+    return (0, -LANE0) if s < 3 else (1, HALF - LANE0)
 
 
 def _levels(span):
@@ -36,21 +43,6 @@
         out.append(cut)
         span = cut
     return out
-
-
-def _groups():
-    out = []
-    for g in range(NQ // 2):
-        first = max((256 * g) // PITCH - SIDE, -2)
-        last = min((256 * g + 255) // PITCH - SIDE, TR + 1)
-        start = first + 2
-        start -= start % 2
-        span = last + 18 + REACH - start + 1
-        out.append((start, span + 2, span))
-    return out
-
-
-GROUPS = _groups()
 
 
 def _split(x):
@@ -186,7 +178,7 @@
 
 
 def _kernel(own_ref, up_ref, down_ref, one_ref, two_ref, w1_ref, bias_ref, w2_ref, out_ref,
-            hs, e3, ef, raw, m1, m2, sq, disp, idx, dat):
+            hs, e3, ef, raw, m1, m2, sq, disp, frac, idx, dat):
     row0, col0 = TR * lax.axis_index("row"), TC * lax.axis_index("col")
     rows, cols = TR * lax.axis_size("row"), TC * lax.axis_size("col")
     lane = lax.broadcasted_iota(jnp.int32, (CH, 128), 1)
@@ -195,13 +187,8 @@
         c = col0 + HALF * h - LANE0 + lane
         col_ok.append((c >= 0) & (c < cols))
     bias = bias_ref[...]
-    moving, fixed, field0, field1 = _windows(
+    moving, fixed, *field = _windows(
         _own(own_ref), up_ref[...], down_ref[...], one_ref[...], two_ref[...])
-    field = [field0[0], field0[1], field1[0], field1[1]]
-
-    def field_row(i):
-        return jnp.concatenate([x[i + 8 - SIDE:i + 9 - SIDE] for x in field] + [jnp.zeros((4, 128), jnp.float32)], axis=0)
-
     def keep(y, h):
         r = row0 + y
         ok = jnp.where((r >= 0) & (r < rows), 1, 0)
@@ -239,87 +226,74 @@
         fixed_rows[h].extend(got)
 
     embed(fixed, -3, FE_BLOCKS, fixed_sink)
-    for h in range(2):
-        cur = jnp.zeros((CH, 128), jnp.float32)
-        q = 0
-        for i in range(36):
-            f0 = PITCH * (i + 1)
-            at, o = f0 // 128, f0 % 128
-            while q < at:
-                ef[h, q] = cur
-                q += 1
-            v = _roll(fixed_rows[h][i + 1], o - (LANE0 - SIDE), 1)
-            cur = jnp.where(lane >= o, v, cur)
-            if o + PITCH > 128:
-                ef[h, q] = cur
-                q += 1
-                cur = v
-        while q < NQ:
-            ef[h, q] = cur
-            q += 1
+    for s in range(SEGS):
+        h, first = _segment(s)
+        for q in range(NQ):
+            cur = None
+            for i in range(4):
+                row = min(max(4 * q - 1 + i, 0), 8 * FE_BLOCKS - 1)
+                v = _roll(fixed_rows[h][row], 32 * i - (WIDE * s - SIDE - first), 1)
+                cur = v if i == 0 else jnp.where(lane < 32 * i, cur, v)
+            ef[s, q] = cur
+
+    moving_rows = [[], []]
 
     def moving_sink(b, h, got):
-        out = []
-        for e0 in got:
-            left, right = _roll(e0, 1, 1), _roll(e0, -1, 1)
-            p1 = 0.5 * (right - left)
-            p2 = 0.5 * (right + left) - e0
-            out += [e0 + 0.25 * p2, p1, p2]
-        hi, lo = _split(jnp.concatenate(out, axis=0))
-        e3[h, 192 * b:192 * b + 192, 0:128] = hi
-        e3[h, 192 * b:192 * b + 192, 128:256] = lo
+        moving_rows[h].extend(got)
 
     embed(moving, -(REACH + 3), ME_BLOCKS, moving_sink)
-
-    cur = jnp.zeros((8, 128), jnp.float32)
-    q = 0
-    for i in range(FROWS):
-        f0 = PITCH * i
-        at, o = f0 // 128, f0 % 128
-        v = _roll(field_row(i), o - (LANE0 - SIDE), 1)
-        cur = jnp.where(lane >= o, v, cur)
-        if o + PITCH > 128:
-            raw[at] = cur
-            cur = v
-            q = at + 1
-    while q < NQ:
-        raw[q] = cur
-        q += 1
+    for r in range(0, PROWS, 2):
+        for s in range(SEGS):
+            h, first = _segment(s)
+            at = WIDE * s - 3 - REACH - first
+            out = []
+            for k in (r, r + 1):
+                e0 = jnp.where(lane < 64, _roll(moving_rows[h][k], -at, 1), _roll(moving_rows[h][k + CUT], 64 - at, 1))
+                left, right = _roll(e0, 1, 1), _roll(e0, -1, 1)
+                p1 = 0.5 * (right - left)
+                p2 = 0.5 * (right + left) - e0
+                out += [e0 + 0.25 * p2, p1, p2]
+            hi, lo = _split(jnp.concatenate(out, axis=0))
+            e3[s, 24 * r:24 * r + 48, 0:128] = hi
+            e3[s, 24 * r:24 * r + 48, 128:256] = lo
+
+    sub = lax.broadcasted_iota(jnp.int32, (8, 128), 0)
+    mine = lane // 32 == sub % 4
+    raw[...] = jnp.zeros_like(raw)
+    for comp in range(2):
+        for b in range(NQ // 2):
+            for s in range(SEGS):
+                h, first = _segment(s)
+                v = field[comp][h][8 * b + 4:8 * b + 12]
+                v = _pick(v, (lane - 32 * (sub % 4) + (WIDE * s - SIDE - first)) & 127)
+                for k in range(2):
+                    raw[comp, 2 * b + k, s:s + 1, :] = jnp.sum(
+                        jnp.where(mine & (sub // 4 == k), v, 0.0), axis=0, keepdims=True)
     m1[...] = jnp.zeros_like(m1)
     m2[...] = jnp.zeros_like(m2)
     dat[...] = jnp.zeros_like(dat)
 
-    sub = lax.broadcasted_iota(jnp.int32, (8, 128), 0)
-    half_at = HALF * (sub % 2)
-
-    def place(q):
-        f = lax.broadcasted_iota(jnp.int32, (8, 128), 1) + 128 * q
-        y = jnp.floor((f.astype(jnp.float32) + 0.5) * (1.0 / PITCH)).astype(jnp.int32)
-        return y - SIDE, f - y * PITCH
-
-    def shifted(x, q, s):
-        if s > 0:
-            a = _roll(x[q], -s, 1)
-            b = _roll(x[min(q + 1, NQ - 1)], -s, 1)
-            return jnp.where(lane < 128 - s, a, b)
-        a = _roll(x[q], -s, 1)
-        b = _roll(x[max(q - 1, 0)], -s, 1)
-        return jnp.where(lane >= -s, a, b)
-
+    j = lane % 32
+    x = col0 + WIDE * sub - SIDE + j
+    col_in = (x >= 0) & (x < cols)
     iota_k = lax.broadcasted_iota(jnp.int32, (128, 256), 0).astype(jnp.float32).astype(jnp.bfloat16)
 
-    def group(g, h):
-        start, count, span = GROUPS[g]
-
-        def pair(ref, s):
-            return jnp.concatenate([jnp.broadcast_to(ref[2 * g + k, s:s + 1, :], (8, 128)) for k in range(2)], axis=1)
-
-        col = jnp.concatenate([idx[2 * g + k, 2 + h:3 + h, :] for k in range(2)], axis=1).astype(jnp.bfloat16)
-        pick = jnp.where(iota_k == jnp.broadcast_to(col, (128, 256)), jnp.bfloat16(1.0), jnp.bfloat16(0.0))
-        t = _dot(e3[h, 24 * start:24 * (start + count), :], jnp.concatenate([pick, pick], axis=0))
-        base = pair(idx, h) - (start * 1.0)
+    def group(q0, s):
+        start = max(4 * q0 - 4, -2) + 2
+
+        def pair(ref, comp, count):
+            return jnp.concatenate(
+                [jnp.broadcast_to(ref[comp, q0 + k, s:s + 1, :], (count, 128)) for k in range(2)], axis=1)
+
+        col = pair(idx, 1, 1) + jnp.where(pair(idx, 0, 1) >= start + CUT, 64.0, 0.0)
+        pick = jnp.where(iota_k == jnp.broadcast_to(col.astype(jnp.bfloat16), (128, 256)),
+                         jnp.bfloat16(1.0), jnp.bfloat16(0.0))
+        count = CUT + 2
+        t = _dot(e3[s, 24 * start:24 * (start + count), :], jnp.concatenate([pick, pick], axis=0))
+        base = pair(idx, 0, 8) - (start * 1.0)
+        base = jnp.where(base >= CUT, base - CUT, base)
         conds = []
-        for cut in _levels(span):
+        for cut in _levels(CUT):
             c = base >= cut
             conds.append((cut, c))
             base = jnp.where(c, base - cut, base)
@@ -329,7 +303,7 @@
             for cut, c in conds:
                 T = [jnp.where(c, T[k + cut], T[k]) if k + cut < len(T) else T[k] for k in range(cut + 2)]
             taps.append(T)
-        fr, fc = pair(disp, 4 + h), pair(disp, 6 + h)
+        fr, fc = pair(frac, 0, 8), pair(frac, 1, 8)
         A, B = [], []
         for a in range(3):
             w = fc * taps[2][a]
@@ -343,55 +317,56 @@
         warped = A[1] + 0.25 * qa + fr * va
         slope_row = va + wa
         slope_col = B[1] + 0.25 * qb + fr * (db + fr * qb)
-        fixed = jnp.concatenate([ef[h, 2 * g], ef[h, 2 * g + 1]], axis=1)
-        miss = (warped - fixed) * (2.0 / CH)
+        target = jnp.concatenate([ef[s, q0], ef[s, q0 + 1]], axis=1)
+        miss = (warped - target) * (2.0 / CH)
         for comp, slope in ((0, slope_row), (1, slope_col)):
             total = jnp.sum(miss * slope, axis=0, keepdims=True)
             for k in range(2):
-                s = 2 * comp + h
-                dat[2 * g + k, s:s + 1, :] = total[:, 128 * k:128 * k + 128]
+                dat[comp, q0 + k, s:s + 1, :] = total[:, 128 * k:128 * k + 128]
 
     def step(t):
         for q in range(NQ):
-            y, j = place(q)
-            c = col0 + half_at + j - SIDE
-            ok = (row0 + y >= 0) & (row0 + y < rows) & (c >= 0) & (c < cols)
-            s = jnp.tanh(raw[q] * (1.0 / REACH))
-            d = REACH * s
-            n = jnp.floor(d + 0.5)
-            sq[q] = s
-            fr = d - n
-            disp[q] = jnp.where(sub < 4, jnp.where(ok, d, 0.0), _roll(fr, 4, 0))
-            first = jnp.where(sub < 2, (y + 18).astype(jnp.float32), (j + (LANE0 - SIDE)).astype(jnp.float32))
-            idx[q] = jnp.maximum(n + first, 0.0)
-        for g in range(NQ // 2 - (t > 0)):
-            for h in range(2):
-                group(g, h)
+            y = 4 * q - 4 + lane // 32
+            ok = col_in & (row0 + y >= 0) & (row0 + y < rows)
+            for comp, origin in ((0, y + REACH + 2), (1, j + REACH)):
+                v = jnp.tanh(raw[comp, q] * (1.0 / REACH))
+                d = REACH * v
+                n = jnp.floor(d + 0.5)
+                sq[comp, q] = v
+                disp[comp, q] = jnp.where(ok, d, 0.0)
+                frac[comp, q] = d - n
+                idx[comp, q] = n + origin.astype(jnp.float32)
+        for q0 in range(0, NQ, 2) if t < 2 else range(1, NQ - 1, 2):
+            for s in range(SEGS):
+                group(q0, s)
         one, two = 1.0 / (1.0 - 0.9 ** (t + 1)), 1.0 / (1.0 - 0.999 ** (t + 1))
-        for q in range(NQ):
-            around = shifted(disp, q, 1) + shifted(disp, q, -1) + shifted(disp, q, PITCH) + shifted(disp, q, -PITCH)
-            s = sq[q]
-            grad = (dat[q] + 2.0 * STIFFNESS * (4.0 * REACH * s - around)) * (1.0 - s * s)
-            a = 0.9 * m1[q] + 0.1 * grad
-            b = 0.999 * m2[q] + 0.001 * grad * grad
-            m1[q] = a
-            m2[q] = b
-            raw[q] = raw[q] - STEP * (a * one) / (jnp.sqrt(b * two) + EPS)
+        for comp in range(2):
+            for q in range(NQ) if t < 2 else range(1, NQ - 1):
+                d = disp[comp, q]
+                up = jnp.where(lane < 96, _roll(d, -32, 1), _roll(disp[comp, min(q + 1, NQ - 1)], -32, 1))
+                down = jnp.where(lane >= 32, _roll(d, 32, 1), _roll(disp[comp, max(q - 1, 0)], 32, 1))
+                around = up + down + _roll(d, 1, 1) + _roll(d, -1, 1)
+                v = sq[comp, q]
+                grad = (dat[comp, q] + 2.0 * STIFFNESS * (4.0 * REACH * v - around)) * (1.0 - v * v)
+                a = 0.9 * m1[comp, q] + 0.1 * grad
+                b = 0.999 * m2[comp, q] + 0.001 * grad * grad
+                m1[comp, q] = a
+                m2[comp, q] = b
+                raw[comp, q] = raw[comp, q] - STEP * (a * one) / (jnp.sqrt(b * two) + EPS)
 
     for t in range(ITERS):
         step(t)
 
-    for y in range(TR):
-        f0 = PITCH * (y + SIDE) + SIDE
-        at, o = f0 // 128, f0 % 128
-        v = raw[at]
-        if o + HALF > 128:
-            v = jnp.where(lane >= o, v, raw[at + 1])
-        v = _roll(v, -o, 1) - _roll(field_row(y + SIDE), -LANE0, 1)
-        w = _roll(v, HALF, 1)
-        for comp in range(2):
-            out_ref[comp, y:y + 1, 0:HALF] = v[2 * comp:2 * comp + 1, 0:HALF]
-            out_ref[comp, y:y + 1, HALF:TC] = w[2 * comp + 1:2 * comp + 2, HALF:TC]
+    own = _own(own_ref)
+    for comp in range(2):
+        for b in range(TR // 8):
+            out = None
+            for s in range(SEGS):
+                v = jnp.where(sub < 4, jnp.broadcast_to(raw[comp, 2 * b + 1, s:s + 1, :], (8, 128)),
+                              jnp.broadcast_to(raw[comp, 2 * b + 2, s:s + 1, :], (8, 128)))
+                v = _pick(v, (lane + 32 * (sub % 4) + (128 + SIDE - WIDE * s)) & 127)
+                out = v if s == 0 else jnp.where(lane < WIDE * s, out, v)
+            out_ref[comp, 8 * b:8 * b + 8] = out - own[2 + comp][8 * b:8 * b + 8]
 
 
 def _swaps(n, first):
@@ -433,9 +408,9 @@
     one, two = _exchange(call(_pack_cols, "pack_cols", [strip, strip], [vmem] * 3, [])(own, up, down), "col")
     return call(_kernel, "refine", [((2, TR, TC), f32)], [vmem] * 8, [
         pltpu.VMEM((2, HROWS * CH, 256), bf16),
-        pltpu.VMEM((2, EROWS * 24, 256), bf16),
-        pltpu.VMEM((2, NQ, CH, 128), f32),
-        *[pltpu.VMEM((NQ, 8, 128), f32) for _ in range(7)],
+        pltpu.VMEM((SEGS, PROWS * 24, 256), bf16),
+        pltpu.VMEM((SEGS, NQ, CH, 128), f32),
+        *[pltpu.VMEM((2, NQ, 8, 128), f32) for _ in range(8)],
     ])(own, up, down, one, two, w1, bias, w2)[0]
 
 

time: 25.2 us -> 23.9 us (0.948)
  Pallas kernels: 12.5 us -> 11.3 us
    pallas_call x1, Pallas kernels: 10.7 us -> 9.42 us  [_local(): call(_kernel, 'refine', [((2, TR, TC), f32)], [vmem] * 8, [pltpu.VMEM((2,...]
where the time goes in v1:
time: 23.9 us; the launch traced here: 23.7 us
  Pallas kernels  11.3 us (47%)
  starting transfers between devices  8.27 us (35%)
  waiting for transfers between devices  4.11 us (17%)
    pallas_call x1, Pallas kernels, _local(): call(_kernel, 'refine', [((2, TR, TC), f32)], [vmem] * 8, [pltpu.VMEM((2,...  9.42 us
    ppermute x4, starting transfers between devices, _exchange(): return [lax.ppermute(x, axis, _swaps(n, k)) for k, x in enumerate(pair)]  8.27 us
    ppermute x4, waiting for transfers between devices, _exchange(): return [lax.ppermute(x, axis, _swaps(n, k)) for k, x in enumerate(pair)]  4.11 us
    pallas_call x1, Pallas kernels, _local(): call(_weights, 'weights', [((128, 48), bf16), ((384, 160), bf16), ((CH, 1...  0.89 us
    pallas_call x1, Pallas kernels, _local(): call(_pack_rows, 'pack_rows', [strip, strip, ((4 * TR, TC), f32)], [anywh...  0.83 us
  transfers between devices with their start and end apart: 4, of which 3 were waited for; matrix products, arithmetic and copies ran while one was open for 0% of the time, Pallas kernels for 4%

profile of v1, /device:TPU:0, one launch (start us, length us, event | category | flops | bytes accessed | tf_op | source)
XLA Modules:
  0.0 23.7 jit_solution(8660490811306535513)
XLA Ops:
  0.0 0.8 %pack_rows.1 = (f32[48,128]{1,0:T(8,128)S(1)}, f32[48,128]{1,0:T(8,128)S(1)}, f32[128,128]{1,0:T(8,128)S(1)}) custom-call(bf16[32,128]{1,0:T(8,128)(2,1)} %mv_ref.1, bf16[32,128]{1,0:T(8,128)(2,1)} %fx_ref.1, f32[2,32,128]{2,1,0:T(8,128)} %fd_ref.1), custom_call_target="tpu_custom_call" | custom-call | tf_op jit(solution)/shard_map/pack_rows/pallas_call | solution.py:399
  0.8 3.0 %collective-permute-start = (f32[48,128]{1,0:T(8,128)S(1)}, f32[48,128]{1,0:T(8,128)S(1)}, u32[]{:S(2)}, u32[]{:S(2)}) collective-permute-start(f32[48,128]{1,0:T(8,128)S(1)} %get-tuple-element.14), channel_id=1, source_target_pairs={{0,8},{8,0},{16,24},{24,16},{1,9},{9,1},{17,25},{25,17},{2,10},{10... | collective-permute-start | bytes 73736 | tf_op jit(solution)/shard_map/ppermute | solution.py:378
  3.8 1.5 %collective-permute-start.1 = (f32[48,128]{1,0:T(8,128)S(1)}, f32[48,128]{1,0:T(8,128)S(1)}, u32[]{:S(2)}, u32[]{:S(2)}) collective-permute-start(f32[48,128]{1,0:T(8,128)S(1)} %get-tuple-element.15), channel_id=1, source_target_pairs={{8,16},{16,8},{24,0},{0,24},{9,17},{17,9},{25,1},{1,25},{10,18},{1... | collective-permute-start | bytes 73736 | tf_op jit(solution)/shard_map/ppermute | solution.py:378
  5.3 0.3 %collective-permute-done.up_ref = f32[48,128]{1,0:T(8,128)S(1)} collective-permute-done((f32[48,128]{1,0:T(8,128)S(1)}, f32[48,128]{1,0:T(8,128)S(1)}, u32[]{:S(2)}, u32[]{:S(2)}) %collective-permute-start) | collective-permute-done | bytes 24608 | tf_op jit(solution)/shard_map/ppermute | solution.py:378
  5.6 2.9 %collective-permute-done.1.down_ref = f32[48,128]{1,0:T(8,128)S(1)} collective-permute-done((f32[48,128]{1,0:T(8,128)S(1)}, f32[48,128]{1,0:T(8,128)S(1)}, u32[]{:S(2)}, u32[]{:S(2)}) %collective-permute-start.1) | collective-permute-done | bytes 24608 | tf_op jit(solution)/shard_map/ppermute | solution.py:378
  8.6 0.0 copy-start
  8.6 0.0 copy-start.1
  8.6 0.1 pack_cols.1
  8.7 0.0 copy-start.2
  8.7 0.1 collective-permute-start.2
  8.8 3.7 %collective-permute-start.3 = (f32[80,128]{1,0:T(8,128)S(1)}, f32[80,128]{1,0:T(8,128)S(1)}, u32[]{:S(2)}, u32[]{:S(2)}) collective-permute-start(f32[80,128]{1,0:T(8,128)S(1)} %get-tuple-element.17), channel_id=1, source_target_pairs={{1,2},{2,1},{3,4},{4,3},{5,6},{6,5},{7,0},{0,7},{9,10},{10,9},{11,... | collective-permute-start | bytes 122888 | tf_op jit(solution)/shard_map/ppermute | solution.py:378
  12.5 0.0 copy-done
  12.5 0.0 copy-done.1
  12.5 0.0 copy-done.2
  12.5 0.9 %weights.1 = (bf16[128,48]{1,0:T(8,128)(2,1)S(1)}, bf16[384,160]{1,0:T(8,128)(2,1)S(1)}, f32[8,128]{1,0:T(8,128)S(1)}) custom-call(f32[8,9]{1,0:T(8,128)S(1)} %copy-done.1, f32[8,8,9]{2,1,0:T(8,128)S(1)} %copy-done, f32[8]{0:T(128)S(1)} %copy-done.2), custom_call_target="tpu_custom_call" | custom-call | tf_op jit(solution)/shard_map/weights/pallas_call | solution.py:403
  13.4 0.0 collective-permute-done.2.one_ref
  13.4 0.9 %collective-permute-done.3.two_ref = f32[80,128]{1,0:T(8,128)S(1)} collective-permute-done((f32[80,128]{1,0:T(8,128)S(1)}, f32[80,128]{1,0:T(8,128)S(1)}, u32[]{:S(2)}, u32[]{:S(2)}) %collective-permute-start.3) | collective-permute-done | bytes 40992 | tf_op jit(solution)/shard_map/ppermute | solution.py:378
  14.3 9.4 %refine.1 = f32[2,32,128]{2,1,0:T(8,128)} custom-call(f32[128,128]{1,0:T(8,128)S(1)} %get-tuple-element.13.own_ref, f32[48,128]{1,0:T(8,128)S(1)} %collective-permute-done.up_ref, f32[48,128]{1,0:T(8,128)S(1)} %collective-permute-done.1.down_ref, f32[80,128]{1,0:T(8,128)S(1)} %collective-permute-done.2.one_ref, ...), custom_call_target="tpu_custom_call" | custom-call | tf_op jit(solution)/shard_map/refine/pallas_call | solution.py:409
Async XLA Ops:
  0.8 4.8 %collective-permute-start = (f32[48,128]{1,0:T(8,128)S(1)}, f32[48,128]{1,0:T(8,128)S(1)}, u32[]{:S(2)}, u32[]{:S(2)}) collective-permute-start(f32[48,128]{1,0:T(8,128)S(1)} %get-tuple-element.14), channel_id=1, source_target_pairs={{0,8},{8,0},{16,24},{24,16},{1,9},{9,1},{17,25},{25,17},{2,10},{10... | collective-permute-start | bytes 73736 | tf_op jit(solution)/shard_map/ppermute | solution.py:378
  3.8 4.7 %collective-permute-start.1 = (f32[48,128]{1,0:T(8,128)S(1)}, f32[48,128]{1,0:T(8,128)S(1)}, u32[]{:S(2)}, u32[]{:S(2)}) collective-permute-start(f32[48,128]{1,0:T(8,128)S(1)} %get-tuple-element.15), channel_id=1, source_target_pairs={{8,16},{16,8},{24,0},{0,24},{9,17},{17,9},{25,1},{1,25},{10,18},{1... | collective-permute-start | bytes 73736 | tf_op jit(solution)/shard_map/ppermute | solution.py:378
  8.6 3.9 %copy-start = (f32[8,8,9]{2,1,0:T(8,128)S(1)}, f32[8,8,9]{2,1,0:T(8,128)}, u32[]{:S(2)}) copy-start(f32[8,8,9]{2,1,0:T(8,128)} %w2_ref.1) | copy-start | bytes 6916
  8.6 3.9 %copy-start.1 = (f32[8,9]{1,0:T(8,128)S(1)}, f32[8,9]{1,0:T(8,128)}, u32[]{:S(2)}) copy-start(f32[8,9]{1,0:T(8,128)} %w1_ref.1) | copy-start | bytes 868
  8.7 3.8 %copy-start.2 = (f32[8]{0:T(128)S(1)}, f32[8]{0:T(128)}, u32[]{:S(2)}) copy-start(f32[8]{0:T(128)} %bias_ref.1) | copy-start | bytes 100
  8.7 4.7 %collective-permute-start.2 = (f32[80,128]{1,0:T(8,128)S(1)}, f32[80,128]{1,0:T(8,128)S(1)}, u32[]{:S(2)}, u32[]{:S(2)}) collective-permute-start(f32[80,128]{1,0:T(8,128)S(1)} %get-tuple-element.16), channel_id=1, source_target_pairs={{0,1},{1,0},{2,3},{3,2},{4,5},{5,4},{6,7},{7,6},{8,9},{9,8},{10,11... | collective-permute-start | bytes 122888 | tf_op jit(solution)/shard_map/ppermute | solution.py:378
  8.8 5.5 %collective-permute-start.3 = (f32[80,128]{1,0:T(8,128)S(1)}, f32[80,128]{1,0:T(8,128)S(1)}, u32[]{:S(2)}, u32[]{:S(2)}) collective-permute-start(f32[80,128]{1,0:T(8,128)S(1)} %get-tuple-element.17), channel_id=1, source_target_pairs={{1,2},{2,1},{3,4},{4,3},{5,6},{6,5},{7,0},{0,7},{9,10},{10,9},{11,... | collective-permute-start | bytes 122888 | tf_op jit(solution)/shard_map/ppermute | solution.py:378

commit v2 on v1

--- a/solution.py
+++ b/solution.py
@@ -13,17 +13,16 @@
 EPS = 0.01
 
 TR, TC = 32, 128
-HALF = 64
 SIDE = 3
 HALO_M = REACH + 1 + 2 + 2
 HALO_PAD = 24
 PADS = (HALO_PAD, 8, 8, 8)
 TALL = TR + 2 * HALO_PAD
-LANE0 = HALO_M
 EROWS = 72
 HROWS = 80
-FE_BLOCKS = 5
-ME_BLOCKS = 9
+TOP = -(REACH + 3)
+BLOCKS = EROWS // 8
+FIXED_BLOCKS = range(2, 7)
 
 SEGS = 5
 WIDE = 26
@@ -32,8 +31,9 @@
 PROWS = EROWS - CUT
 
 
-def _segment(s):
-    return (0, -LANE0) if s < 3 else (1, HALF - LANE0)
+FROM0 = REACH + 3
+AT4 = 62
+FROM4 = WIDE * (SEGS - 1) - FROM0 - AT4
 
 
 def _levels(span):
@@ -145,7 +145,7 @@
     m2_ref[...] = jnp.concatenate(hi_rows + lo_rows, axis=0)[:, :160].astype(jnp.bfloat16)
 
 
-def _pack_cols(own_ref, up_ref, down_ref, one_ref, two_ref):
+def _pack_cols(own_ref, up_ref, down_ref, _, one_ref, two_ref):
     even = lax.rem(lax.axis_index("col"), 2) == 0
     tall = _tall(_own(own_ref), up_ref[...], down_ref[...])
     lane = lax.broadcasted_iota(jnp.int32, (8, 128), 1)
@@ -161,114 +161,133 @@
         two_ref[8 * i:8 * i + 8] = jnp.where(even, first, last)
 
 
-def _windows(own, up, down, one, two):
+def _strips(own, up, down, one, two):
     c, n = lax.axis_index("col"), lax.axis_size("col")
     even = lax.rem(c, 2) == 0
     left = jnp.where(c > 0, jnp.where(even, two, one), 0.0)
     right = jnp.where(c < n - 1, jnp.where(even, one, two), 0.0)
     out = []
-    end = HALO_M - HALF + TC
     for k, x in enumerate(_tall(own, up, down)):
         lane = lax.broadcasted_iota(jnp.int32, x.shape, 1)
         r = x.shape[0]
-        lw = jnp.where(lane < HALO_M, _roll(left[:r], -32 * k, 1), _roll(x, HALO_M, 1))
-        rw = jnp.where(lane < end, _roll(x, HALO_M - HALF, 1), _roll(right[:r], end - 32 * k, 1))
-        out.append((lw, rw))
+        v = jnp.where(lane < TC - FROM4, _roll(x, -FROM4, 1), _roll(right[:r], TC - FROM4 - 32 * k, 1))
+        v = jnp.where(lane < AT4, _roll(x, FROM0, 1), v)
+        out.append(jnp.where((lane < FROM0) | (lane >= 126), _roll(left[:r], FROM0 - HALO_M - 32 * k, 1), v))
     return out
 
 
-def _kernel(own_ref, up_ref, down_ref, one_ref, two_ref, w1_ref, bias_ref, w2_ref, out_ref,
-            hs, e3, ef, raw, m1, m2, sq, disp, frac, idx, dat):
-    row0, col0 = TR * lax.axis_index("row"), TC * lax.axis_index("col")
-    rows, cols = TR * lax.axis_size("row"), TC * lax.axis_size("col")
-    lane = lax.broadcasted_iota(jnp.int32, (CH, 128), 1)
-    col_ok = []
-    for h in range(2):
-        c = col0 + HALF * h - LANE0 + lane
-        col_ok.append((c >= 0) & (c < cols))
+class _Place:
+    def __init__(self):
+        self.row, self.col = TR * lax.axis_index("row"), TC * lax.axis_index("col")
+        self.rows, self.cols = TR * lax.axis_size("row"), TC * lax.axis_size("col")
+
+    def keep(self, y, col_ok):
+        r = self.row + y
+        ok = jnp.where((r >= 0) & (r < self.rows), 1, 0)
+        return jnp.where(col_ok, ok.astype(jnp.float32), 0.0)
+
+
+def _embed(place, moving, fixed, column, w1_ref, bias_ref, w2_ref, hs, sink):
     bias = bias_ref[...]
-    moving, fixed, *field = _windows(
-        _own(own_ref), up_ref[...], down_ref[...], one_ref[...], two_ref[...])
-    def keep(y, h):
-        r = row0 + y
-        ok = jnp.where((r >= 0) & (r < rows), 1, 0)
-        return jnp.where(col_ok[h], ok.astype(jnp.float32), 0.0)
-
-    def embed(image, top, blocks, sink):
-        shifted = [jnp.concatenate([_roll(image[h], 1 - kx, 1) for h in range(2)], axis=1) for kx in range(3)]
-        known = image[0].shape[0]
-        for b in range(blocks + 1):
-            if 8 * b + 16 > known:
-                for k in range(8 * b, 8 * blocks + 2, 2):
-                    hs[0, CH * k:CH * k + 16] = jnp.zeros((16, 256), jnp.bfloat16)
-                    hs[1, CH * k:CH * k + 16] = jnp.zeros((16, 256), jnp.bfloat16)
-                break
-            t = _dot(w1_ref[...], jnp.concatenate([x[8 * b:8 * b + 16] for x in shifted], axis=0).astype(jnp.bfloat16))
-            pre = t[:64] + t[64:]
-            for h in range(2):
-                v = jnp.concatenate([
-                    jnp.maximum(pre[CH * k:CH * k + CH, 128 * h:128 * h + 128] + bias, 0.0) * keep(top - 1 + 8 * b + k, h)
-                    for k in range(8)], axis=0)
-                hi, lo = _split(v)
-                hs[0, 64 * b:64 * b + 64, 128 * h:128 * h + 128] = hi
-                hs[1, 64 * b:64 * b + 64, 128 * h:128 * h + 128] = lo
-        for b in range(blocks):
-            t = _dot(w2_ref[...], jnp.concatenate([hs[0, 64 * b:64 * b + 80], hs[1, 64 * b:64 * b + 80]], axis=0))
-            v = t[:192] + t[192:]
-            for h in range(2):
-                o = [v[64 * kx:64 * kx + 64, 128 * h:128 * h + 128] for kx in range(3)]
-                e = o[1] + _roll(o[0], 1, 1) + _roll(o[2], -1, 1)
-                sink(b, h, [e[CH * k:CH * k + CH] * keep(top + 8 * b + k, h) for k in range(8)])
-
-    fixed_rows = [[], []]
-
-    def fixed_sink(b, h, got):
-        fixed_rows[h].extend(got)
-
-    embed(fixed, -3, FE_BLOCKS, fixed_sink)
-    for s in range(SEGS):
-        h, first = _segment(s)
-        for q in range(NQ):
-            cur = None
-            for i in range(4):
-                row = min(max(4 * q - 1 + i, 0), 8 * FE_BLOCKS - 1)
-                v = _roll(fixed_rows[h][row], 32 * i - (WIDE * s - SIDE - first), 1)
-                cur = v if i == 0 else jnp.where(lane < 32 * i, cur, v)
-            ef[s, q] = cur
-
-    moving_rows = [[], []]
-
-    def moving_sink(b, h, got):
-        moving_rows[h].extend(got)
-
-    embed(moving, -(REACH + 3), ME_BLOCKS, moving_sink)
-    for r in range(0, PROWS, 2):
-        for s in range(SEGS):
-            h, first = _segment(s)
-            at = WIDE * s - 3 - REACH - first
-            out = []
-            for k in (r, r + 1):
-                e0 = jnp.where(lane < 64, _roll(moving_rows[h][k], -at, 1), _roll(moving_rows[h][k + CUT], 64 - at, 1))
-                left, right = _roll(e0, 1, 1), _roll(e0, -1, 1)
-                p1 = 0.5 * (right - left)
-                p2 = 0.5 * (right + left) - e0
-                out += [e0 + 0.25 * p2, p1, p2]
-            hi, lo = _split(jnp.concatenate(out, axis=0))
-            e3[s, 24 * r:24 * r + 48, 0:128] = hi
-            e3[s, 24 * r:24 * r + 48, 128:256] = lo
-
+    x = place.col + column
+    col_ok = (x >= 0) & (x < place.cols)
+    blank = jnp.zeros((16, 128), jnp.float32)
+    image = [moving, jnp.concatenate([blank, fixed, blank], axis=0)]
+    shifted = [jnp.concatenate([_roll(v, 1 - kx, 1) for v in image], axis=1) for kx in range(3)]
+    hs[:, 8 * 72:, :] = jnp.zeros((2, 64, 256), jnp.bfloat16)
+    for b in range(BLOCKS):
+        t = _dot(w1_ref[...], jnp.concatenate([v[8 * b:8 * b + 16] for v in shifted], axis=0).astype(jnp.bfloat16))
+        pre = t[:64] + t[64:]
+        for h in range(2):
+            at = slice(128 * h, 128 * h + 128)
+            if h == 1 and b not in FIXED_BLOCKS:
+                hs[:, 64 * b:64 * b + 64, at] = jnp.zeros((2, 64, 128), jnp.bfloat16)
+                continue
+            v = jnp.concatenate([
+                jnp.maximum(pre[CH * k:CH * k + CH, at] + bias, 0.0) * place.keep(TOP - 1 + 8 * b + k, col_ok)
+                for k in range(8)], axis=0)
+            hs[0, 64 * b:64 * b + 64, at], hs[1, 64 * b:64 * b + 64, at] = _split(v)
+    for b in range(BLOCKS):
+        t = _dot(w2_ref[...], jnp.concatenate([hs[0, 64 * b:64 * b + 80], hs[1, 64 * b:64 * b + 80]], axis=0))
+        v = t[:192] + t[192:]
+        for h in range(2):
+            if h == 1 and b not in FIXED_BLOCKS:
+                continue
+            o = [v[64 * kx:64 * kx + 64, 128 * h:128 * h + 128] for kx in range(3)]
+            e = o[1] + _roll(o[0], 1, 1) + _roll(o[2], -1, 1)
+            sink(b, h, [e[CH * k:CH * k + CH] * place.keep(TOP + 8 * b + k, col_ok) for k in range(8)])
+
+
+def _build(moving, fixed, field, window, pixel, s, e3, ef, raw):
+    lane = lax.broadcasted_iota(jnp.int32, (8, 128), 1)
     sub = lax.broadcasted_iota(jnp.int32, (8, 128), 0)
     mine = lane // 32 == sub % 4
-    raw[...] = jnp.zeros_like(raw)
+    for r in range(0, PROWS, 2):
+        out = []
+        for k in (r, r + 1):
+            e0 = jnp.where(lane < 64, _roll(moving[k], -window, 1), _roll(moving[k + CUT], 64 - window, 1))
+            left, right = _roll(e0, 1, 1), _roll(e0, -1, 1)
+            p1 = 0.5 * (right - left)
+            p2 = 0.5 * (right + left) - e0
+            out += [e0 + 0.25 * p2, p1, p2]
+        hi, lo = _split(jnp.concatenate(out, axis=0))
+        e3[24 * r:24 * r + 48, 0:128] = hi
+        e3[24 * r:24 * r + 48, 128:256] = lo
+    for q in range(NQ):
+        cur = None
+        for i in range(4):
+            row = min(max(4 * q - 4 + i, -2), TR + 1) - TOP
+            v = _roll(fixed[row], 32 * i - pixel, 1)
+            cur = v if i == 0 else jnp.where(lane < 32 * i, cur, v)
+        ef[q] = cur
     for comp in range(2):
         for b in range(NQ // 2):
-            for s in range(SEGS):
-                h, first = _segment(s)
-                v = field[comp][h][8 * b + 4:8 * b + 12]
-                v = _pick(v, (lane - 32 * (sub % 4) + (WIDE * s - SIDE - first)) & 127)
-                for k in range(2):
-                    raw[comp, 2 * b + k, s:s + 1, :] = jnp.sum(
-                        jnp.where(mine & (sub // 4 == k), v, 0.0), axis=0, keepdims=True)
+            v = field[comp][8 * b + 4:8 * b + 12]
+            v = _pick(v, (lane - 32 * (sub % 4) + pixel) & 127)
+            for k in range(2):
+                raw[comp, 2 * b + k, s:s + 1, :] = jnp.sum(
+                    jnp.where(mine & (sub // 4 == k), v, 0.0), axis=0, keepdims=True)
+
+
+def _middle(own_ref, up_ref, down_ref, w1_ref, bias_ref, w2_ref, e3_ref, ef_ref, raw_ref, rows_ref, hs):
+    moving, fixed, *field = _tall(_own(own_ref), up_ref[...], down_ref[...])
+    lane = lax.broadcasted_iota(jnp.int32, (CH, 128), 1)
+    rows = [{}, {}]
+
+    def sink(b, h, got):
+        for k, v in enumerate(got):
+            rows[h][8 * b + k] = v
+            rows_ref[h, 8 * b + k] = v
+
+    _embed(_Place(), moving, fixed, lane, w1_ref, bias_ref, w2_ref, hs, sink)
+    raw_ref[...] = jnp.zeros_like(raw_ref)
+    for s in range(1, SEGS - 1):
+        _build(rows[0], rows[1], field, WIDE * s - 3 - REACH, WIDE * s - SIDE, s,
+               e3_ref.at[s - 1], ef_ref.at[s - 1], raw_ref)
+
+
+def _refine(own_ref, up_ref, down_ref, one_ref, two_ref, w1_ref, bias_ref, w2_ref, mid3_ref, midf_ref, midr_ref, rows_ref,
+            out_ref, hs, e3, ef, raw, m1, m2, sq, disp, frac, idx, dat):
+    place = _Place()
+    row0, col0, rows, cols = place.row, place.col, place.rows, place.cols
+    lane = lax.broadcasted_iota(jnp.int32, (8, 128), 1)
+    sub = lax.broadcasted_iota(jnp.int32, (8, 128), 0)
+    moving, fixed, *field = _strips(_own(own_ref), up_ref[...], down_ref[...], one_ref[...], two_ref[...])
+    column = jnp.where(lane < AT4, lane - FROM0, jnp.where(lane < 126, lane + FROM4, lane - 126 - HALO_M))
+    edge = [[{}, {}], [{}, {}]]
+
+    def sink(b, h, got):
+        for k, v in enumerate(got):
+            mine = rows_ref[h, 8 * b + k]
+            edge[0][h][8 * b + k] = jnp.where(lane < 30, v, _roll(mine, FROM0, 1))
+            edge[1][h][8 * b + k] = jnp.where(lane < 90, _roll(mine, -FROM4, 1), v)
+
+    _embed(place, moving, fixed, column, w1_ref, bias_ref, w2_ref, hs, sink)
+    raw[...] = midr_ref[...]
+    _build(edge[0][0], edge[0][1], field, 0, REACH, 0, e3.at[0], ef.at[0], raw)
+    _build(edge[1][0], edge[1][1], field, AT4, AT4 + REACH, SEGS - 1, e3.at[1], ef.at[1], raw)
+    tables = [e3.at[0]] + [mid3_ref.at[k] for k in range(SEGS - 2)] + [e3.at[1]]
+    targets = [ef.at[0]] + [midf_ref.at[k] for k in range(SEGS - 2)] + [ef.at[1]]
     m1[...] = jnp.zeros_like(m1)
     m2[...] = jnp.zeros_like(m2)
     dat[...] = jnp.zeros_like(dat)
@@ -289,7 +308,7 @@
         pick = jnp.where(iota_k == jnp.broadcast_to(col.astype(jnp.bfloat16), (128, 256)),
                          jnp.bfloat16(1.0), jnp.bfloat16(0.0))
         count = CUT + 2
-        t = _dot(e3[s, 24 * start:24 * (start + count), :], jnp.concatenate([pick, pick], axis=0))
+        t = _dot(tables[s][24 * start:24 * (start + count), :], jnp.concatenate([pick, pick], axis=0))
         base = pair(idx, 0, 8) - (start * 1.0)
         base = jnp.where(base >= CUT, base - CUT, base)
         conds = []
@@ -317,7 +336,7 @@
         warped = A[1] + 0.25 * qa + fr * va
         slope_row = va + wa
         slope_col = B[1] + 0.25 * qb + fr * (db + fr * qb)
-        target = jnp.concatenate([ef[s, q0], ef[s, q0 + 1]], axis=1)
+        target = jnp.concatenate([targets[s][q0], targets[s][q0 + 1]], axis=1)
         miss = (warped - target) * (2.0 / CH)
         for comp, slope in ((0, slope_row), (1, slope_col)):
             total = jnp.sum(miss * slope, axis=0, keepdims=True)
@@ -405,13 +424,16 @@
         pltpu.VMEM((CH, 9), f32), pltpu.VMEM((CH, CH, 9), f32), pltpu.VMEM((2, CH, 128), f32),
         pltpu.SemaphoreType.DMA((2,))])(first_weight, second_weight, first_bias)
     strip = ((TALL, 128), f32)
-    one, two = _exchange(call(_pack_cols, "pack_cols", [strip, strip], [vmem] * 3, [])(own, up, down), "col")
-    return call(_kernel, "refine", [((2, TR, TC), f32)], [vmem] * 8, [
-        pltpu.VMEM((2, HROWS * CH, 256), bf16),
-        pltpu.VMEM((SEGS, PROWS * 24, 256), bf16),
-        pltpu.VMEM((SEGS, NQ, CH, 128), f32),
+    one, two = _exchange(call(_pack_cols, "pack_cols", [strip, strip], [vmem] * 4, [])(own, up, down, bias), "col")
+    hidden = pltpu.VMEM((2, HROWS * CH, 256), bf16)
+    table, target = (PROWS * 24, 256), (NQ, CH, 128)
+    mid = call(_middle, "middle", [
+        ((SEGS - 2,) + table, bf16), ((SEGS - 2,) + target, f32), ((2, NQ, 8, 128), f32), ((2, EROWS, CH, 128), f32),
+    ], [vmem] * 6, [hidden])(own, up, down, w1, bias, w2)
+    return call(_refine, "refine", [((2, TR, TC), f32)], [vmem] * 12, [
+        hidden, pltpu.VMEM((2,) + table, bf16), pltpu.VMEM((2,) + target, f32),
         *[pltpu.VMEM((2, NQ, 8, 128), f32) for _ in range(8)],
-    ])(own, up, down, one, two, w1, bias, w2)[0]
+    ])(own, up, down, one, two, w1, bias, w2, *mid)[0]
 
 
 def solution(mesh):

time: 23.9 us -> 22.9 us (0.958)
  waiting for transfers between devices: 4.11 us -> 0.27 us
  local copies, waits for them, and re-layouts: 0.01 us -> 2.1 us
  Pallas kernels: 11.3 us -> 11.9 us
    ppermute x4, waiting for transfers between devices: 4.11 us -> 0.27 us  [_exchange(): return [lax.ppermute(x, axis, _swaps(n, k)) for k, x in enumerate(pair)]]
    unnamed x6, local copies, waits for them, and re-layouts: 0.01 us -> 2.1 us
    pallas_call x2 -> x3, Pallas kernels: 9.54 us -> 10.2 us  [the longest x1 8.31 us: _local(): call(_refine, 'refine', [((2, TR, TC), f32)], [vmem] * 12, [hidden, pltpu...]
  transfers between devices with their start and end apart: 4 -> 4, of which waited for: 3 -> 1; matrix products, arithmetic and copies ran while one was open for 0% -> 0% of each run, Pallas kernels for 4% -> 12%
where the time goes in v2:
time: 22.9 us; the launch traced here: 22.6 us
  Pallas kernels  11.9 us (52%)
  starting transfers between devices  8.27 us (36%)
  local copies, waits for them, and re-layouts  2.1 us (9%)
  waiting for transfers between devices  0.27 us (1%)
    pallas_call x1, Pallas kernels, _local(): call(_refine, 'refine', [((2, TR, TC), f32)], [vmem] * 12, [hidden, pltpu...  8.31 us
    ppermute x4, starting transfers between devices, _exchange(): return [lax.ppermute(x, axis, _swaps(n, k)) for k, x in enumerate(pair)]  8.27 us
    unnamed x6, local copies, waits for them, and re-layouts  2.1 us
    pallas_call x1, Pallas kernels, _local(): call(_middle, 'middle', [((SEGS - 2,) + table, bf16), ((SEGS - 2,) + targ...  1.73 us
    pallas_call x1, Pallas kernels, _local(): call(_weights, 'weights', [((128, 48), bf16), ((384, 160), bf16), ((CH, 1...  0.89 us
    pallas_call x1, Pallas kernels, _local(): call(_pack_rows, 'pack_rows', [strip, strip, ((4 * TR, TC), f32)], [anywh...  0.83 us
  transfers between devices with their start and end apart: 4, of which 1 were waited for; matrix products, arithmetic and copies ran while one was open for 0% of the time, Pallas kernels for 12%

profile of v2, /device:TPU:0, one launch (start us, length us, event | category | flops | bytes accessed | tf_op | source)
XLA Modules:
  0.0 22.6 jit_solution(5411959673913791959)
XLA Ops:
  0.0 0.8 %pack_rows.1 = (f32[48,128]{1,0:T(8,128)S(1)}, f32[48,128]{1,0:T(8,128)S(1)}, f32[128,128]{1,0:T(8,128)S(1)}) custom-call(bf16[32,128]{1,0:T(8,128)(2,1)} %mv_ref.1, bf16[32,128]{1,0:T(8,128)(2,1)} %fx_ref.1, f32[2,32,128]{2,1,0:T(8,128)} %fd_ref.1), custom_call_target="tpu_custom_call" | custom-call | tf_op jit(solution)/shard_map/pack_rows/pallas_call | solution.py:418
  0.8 3.0 %collective-permute-start = (f32[48,128]{1,0:T(8,128)S(1)}, f32[48,128]{1,0:T(8,128)S(1)}, u32[]{:S(2)}, u32[]{:S(2)}) collective-permute-start(f32[48,128]{1,0:T(8,128)S(1)} %get-tuple-element.18), channel_id=1, source_target_pairs={{0,8},{8,0},{16,24},{24,16},{1,9},{9,1},{17,25},{25,17},{2,10},{10... | collective-permute-start | bytes 73736 | tf_op jit(solution)/shard_map/ppermute | solution.py:397
  3.8 1.5 %collective-permute-start.1 = (f32[48,128]{1,0:T(8,128)S(1)}, f32[48,128]{1,0:T(8,128)S(1)}, u32[]{:S(2)}, u32[]{:S(2)}) collective-permute-start(f32[48,128]{1,0:T(8,128)S(1)} %get-tuple-element.19), channel_id=1, source_target_pairs={{8,16},{16,8},{24,0},{0,24},{9,17},{17,9},{25,1},{1,25},{10,18},{1... | collective-permute-start | bytes 73736 | tf_op jit(solution)/shard_map/ppermute | solution.py:397
  5.3 0.0 copy-start
  5.3 0.8 %copy-done = f32[8,8,9]{2,1,0:T(8,128)S(1)} copy-done((f32[8,8,9]{2,1,0:T(8,128)S(1)}, f32[8,8,9]{2,1,0:T(8,128)}, u32[]{:S(2)}) %copy-start) | copy-done | bytes 2328
  6.1 0.0 copy-start.1
  6.1 0.7 %copy-done.1 = f32[8,9]{1,0:T(8,128)S(1)} copy-done((f32[8,9]{1,0:T(8,128)S(1)}, f32[8,9]{1,0:T(8,128)}, u32[]{:S(2)}) %copy-start.1) | copy-done | bytes 312
  6.8 0.0 copy-start.2
  6.8 0.7 %copy-done.2 = f32[8]{0:T(128)S(1)} copy-done((f32[8]{0:T(128)S(1)}, f32[8]{0:T(128)}, u32[]{:S(2)}) %copy-start.2) | copy-done | bytes 56
  7.4 0.9 %weights.1 = (bf16[128,48]{1,0:T(8,128)(2,1)S(1)}, bf16[384,160]{1,0:T(8,128)(2,1)S(1)}, f32[8,128]{1,0:T(8,128)S(1)}) custom-call(f32[8,9]{1,0:T(8,128)S(1)} %copy-done.1, f32[8,8,9]{2,1,0:T(8,128)S(1)} %copy-done, f32[8]{0:T(128)S(1)} %copy-done.2), custom_call_target="tpu_custom_call" | custom-call | tf_op jit(solution)/shard_map/weights/pallas_call | solution.py:422
  8.3 0.0 collective-permute-done.up_ref
  8.3 0.2 collective-permute-done.1.down_ref
  8.6 0.1 pack_cols.1
  8.7 0.1 collective-permute-start.2
  8.8 3.7 %collective-permute-start.3 = (f32[80,128]{1,0:T(8,128)S(1)}, f32[80,128]{1,0:T(8,128)S(1)}, u32[]{:S(2)}, u32[]{:S(2)}) collective-permute-start(f32[80,128]{1,0:T(8,128)S(1)} %get-tuple-element.22), channel_id=1, source_target_pairs={{1,2},{2,1},{3,4},{4,3},{5,6},{6,5},{7,0},{0,7},{9,10},{10,9},{11,... | collective-permute-start | bytes 122888 | tf_op jit(solution)/shard_map/ppermute | solution.py:397
  12.5 1.7 %middle.1 = (bf16[3,1248,256]{2,1,0:T(8,128)(2,1)S(1)}, f32[3,10,8,128]{3,2,1,0:T(8,128)S(1)}, f32[2,10,8,128]{3,2,1,0:T(8,128)S(1)}, f32[2,72,8,128]{3,2,1,0:T(8,128)S(1)}) custom-call(f32[128,128]{1,0:T(8,128)S(1)} %get-tuple-element.17.own_ref, f32[48,128]{1,0:T(8,128)S(1)} %collective-permute-done.up_ref, f32[48,128]{1,0:T(8,128)S(1)} %collective-permute-done.1.down_ref, ...), custom_call_target="tpu_custom_call" | custom-call | tf_op jit(solution)/shard_map/middle/pallas_call | solution.py:430
  14.2 0.0 collective-permute-done.2.one_ref
  14.2 0.0 collective-permute-done.3.two_ref
  14.3 8.3 %refine.1 = f32[2,32,128]{2,1,0:T(8,128)} custom-call(f32[128,128]{1,0:T(8,128)S(1)} %get-tuple-element.17.own_ref, f32[48,128]{1,0:T(8,128)S(1)} %collective-permute-done.up_ref, f32[48,128]{1,0:T(8,128)S(1)} %collective-permute-done.1.down_ref, f32[80,128]{1,0:T(8,128)S(1)} %collective-permute-done.2.one_ref, ...), custom_call_target="tpu_custom_call" | custom-call | tf_op jit(solution)/shard_map/refine/pallas_call | solution.py:433
Async XLA Ops:
  0.8 7.5 %collective-permute-start = (f32[48,128]{1,0:T(8,128)S(1)}, f32[48,128]{1,0:T(8,128)S(1)}, u32[]{:S(2)}, u32[]{:S(2)}) collective-permute-start(f32[48,128]{1,0:T(8,128)S(1)} %get-tuple-element.18), channel_id=1, source_target_pairs={{0,8},{8,0},{16,24},{24,16},{1,9},{9,1},{17,25},{25,17},{2,10},{10... | collective-permute-start | bytes 73736 | tf_op jit(solution)/shard_map/ppermute | solution.py:397
  3.8 4.7 %collective-permute-start.1 = (f32[48,128]{1,0:T(8,128)S(1)}, f32[48,128]{1,0:T(8,128)S(1)}, u32[]{:S(2)}, u32[]{:S(2)}) collective-permute-start(f32[48,128]{1,0:T(8,128)S(1)} %get-tuple-element.19), channel_id=1, source_target_pairs={{8,16},{16,8},{24,0},{0,24},{9,17},{17,9},{25,1},{1,25},{10,18},{1... | collective-permute-start | bytes 73736 | tf_op jit(solution)/shard_map/ppermute | solution.py:397
  5.3 0.8 %copy-start = (f32[8,8,9]{2,1,0:T(8,128)S(1)}, f32[8,8,9]{2,1,0:T(8,128)}, u32[]{:S(2)}) copy-start(f32[8,8,9]{2,1,0:T(8,128)} %w2_ref.1) | copy-start | bytes 6916
  6.1 0.7 %copy-start.1 = (f32[8,9]{1,0:T(8,128)S(1)}, f32[8,9]{1,0:T(8,128)}, u32[]{:S(2)}) copy-start(f32[8,9]{1,0:T(8,128)} %w1_ref.1) | copy-start | bytes 868
  6.8 0.7 %copy-start.2 = (f32[8]{0:T(128)S(1)}, f32[8]{0:T(128)}, u32[]{:S(2)}) copy-start(f32[8]{0:T(128)} %bias_ref.1) | copy-start | bytes 100
  8.7 5.5 %collective-permute-start.2 = (f32[80,128]{1,0:T(8,128)S(1)}, f32[80,128]{1,0:T(8,128)S(1)}, u32[]{:S(2)}, u32[]{:S(2)}) collective-permute-start(f32[80,128]{1,0:T(8,128)S(1)} %get-tuple-element.21), channel_id=1, source_target_pairs={{0,1},{1,0},{2,3},{3,2},{4,5},{5,4},{6,7},{7,6},{8,9},{9,8},{10,11... | collective-permute-start | bytes 122888 | tf_op jit(solution)/shard_map/ppermute | solution.py:397
  8.8 5.5 %collective-permute-start.3 = (f32[80,128]{1,0:T(8,128)S(1)}, f32[80,128]{1,0:T(8,128)S(1)}, u32[]{:S(2)}, u32[]{:S(2)}) collective-permute-start(f32[80,128]{1,0:T(8,128)S(1)} %get-tuple-element.22), channel_id=1, source_target_pairs={{1,2},{2,1},{3,4},{4,3},{5,6},{6,5},{7,0},{0,7},{9,10},{10,9},{11,... | collective-permute-start | bytes 122888 | tf_op jit(solution)/shard_map/ppermute | solution.py:397

commit v3 on v2

--- a/solution.py
+++ b/solution.py
@@ -32,6 +32,9 @@
 
 
 FROM0 = REACH + 3
+FAR = 117
+PACE = 600
+HALF = 5
 AT4 = 62
 FROM4 = WIDE * (SEGS - 1) - FROM0 - AT4
 
@@ -161,18 +164,30 @@
         two_ref[8 * i:8 * i + 8] = jnp.where(even, first, last)
 
 
-def _strips(own, up, down, one, two):
+def _edges(own, up, down, one, two):
     c, n = lax.axis_index("col"), lax.axis_size("col")
     even = lax.rem(c, 2) == 0
     left = jnp.where(c > 0, jnp.where(even, two, one), 0.0)
     right = jnp.where(c < n - 1, jnp.where(even, one, two), 0.0)
-    out = []
-    for k, x in enumerate(_tall(own, up, down)):
+    tall = _tall(own, up, down)
+    images = []
+    for k, x in enumerate(tall[:2]):
+        lane = lax.broadcasted_iota(jnp.int32, x.shape, 1) - 64 * k
+        r = x.shape[0]
+        v = jnp.where(lane < 32 + TC - FAR, _roll(x, 64 * k + 32 - FAR, 1), _roll(right[:r], 32 * k + 32 + TC - FAR, 1))
+        v = jnp.where(lane < 32, _roll(x, 64 * k + HALO_M, 1), v)
+        images.append(jnp.where(lane < HALO_M, _roll(left[:r], 32 * k, 1), v))
+    blank = jnp.zeros((16, 128), jnp.float32)
+    fixed = jnp.concatenate([blank, images[1], blank], axis=0)
+    lane = lax.broadcasted_iota(jnp.int32, fixed.shape, 1)
+    out = [jnp.where(lane < 64, images[0], fixed)]
+    for k in (2, 3):
+        x = tall[k]
         lane = lax.broadcasted_iota(jnp.int32, x.shape, 1)
         r = x.shape[0]
         v = jnp.where(lane < TC - FROM4, _roll(x, -FROM4, 1), _roll(right[:r], TC - FROM4 - 32 * k, 1))
         v = jnp.where(lane < AT4, _roll(x, FROM0, 1), v)
-        out.append(jnp.where((lane < FROM0) | (lane >= 126), _roll(left[:r], FROM0 - HALO_M - 32 * k, 1), v))
+        out.append(jnp.where(lane < FROM0, _roll(left[:r], FROM0 - HALO_M - 32 * k, 1), v))
     return out
 
 
@@ -187,41 +202,42 @@
         return jnp.where(col_ok, ok.astype(jnp.float32), 0.0)
 
 
-def _embed(place, moving, fixed, column, w1_ref, bias_ref, w2_ref, hs, sink):
+def _embed(place, images, column, tops, blocks, w1_ref, bias_ref, w2_ref, hs, sink):
     bias = bias_ref[...]
     x = place.col + column
     col_ok = (x >= 0) & (x < place.cols)
-    blank = jnp.zeros((16, 128), jnp.float32)
-    image = [moving, jnp.concatenate([blank, fixed, blank], axis=0)]
-    shifted = [jnp.concatenate([_roll(v, 1 - kx, 1) for v in image], axis=1) for kx in range(3)]
-    hs[:, 8 * 72:, :] = jnp.zeros((2, 64, 256), jnp.bfloat16)
-    for b in range(BLOCKS):
+    shifted = [jnp.concatenate([_roll(v, 1 - kx, 1) for v in images], axis=1) for kx in range(3)]
+    count = max(max(b) for b in blocks) + 1
+    for b in range(count + 1):
+        if 8 * b + 16 > shifted[0].shape[0]:
+            hs[:, 64 * b:64 * b + 64, :] = jnp.zeros((2, 64, 256), jnp.bfloat16)
+            continue
         t = _dot(w1_ref[...], jnp.concatenate([v[8 * b:8 * b + 16] for v in shifted], axis=0).astype(jnp.bfloat16))
         pre = t[:64] + t[64:]
         for h in range(2):
             at = slice(128 * h, 128 * h + 128)
-            if h == 1 and b not in FIXED_BLOCKS:
+            if b not in blocks[h] and b - 1 not in blocks[h]:
                 hs[:, 64 * b:64 * b + 64, at] = jnp.zeros((2, 64, 128), jnp.bfloat16)
                 continue
             v = jnp.concatenate([
-                jnp.maximum(pre[CH * k:CH * k + CH, at] + bias, 0.0) * place.keep(TOP - 1 + 8 * b + k, col_ok)
+                jnp.maximum(pre[CH * k:CH * k + CH, at] + bias, 0.0) * place.keep(tops[h] - 1 + 8 * b + k, col_ok)
                 for k in range(8)], axis=0)
             hs[0, 64 * b:64 * b + 64, at], hs[1, 64 * b:64 * b + 64, at] = _split(v)
-    for b in range(BLOCKS):
+        yield 200
+    for b in range(count):
         t = _dot(w2_ref[...], jnp.concatenate([hs[0, 64 * b:64 * b + 80], hs[1, 64 * b:64 * b + 80]], axis=0))
         v = t[:192] + t[192:]
         for h in range(2):
-            if h == 1 and b not in FIXED_BLOCKS:
+            if b not in blocks[h]:
                 continue
             o = [v[64 * kx:64 * kx + 64, 128 * h:128 * h + 128] for kx in range(3)]
             e = o[1] + _roll(o[0], 1, 1) + _roll(o[2], -1, 1)
-            sink(b, h, [e[CH * k:CH * k + CH] * place.keep(TOP + 8 * b + k, col_ok) for k in range(8)])
-
-
-def _build(moving, fixed, field, window, pixel, s, e3, ef, raw):
+            sink(b, h, [e[CH * k:CH * k + CH] * place.keep(tops[h] + 8 * b + k, col_ok) for k in range(8)])
+        yield 250
+
+
+def _build(moving, fixed, window, pixel, e3, ef):
     lane = lax.broadcasted_iota(jnp.int32, (8, 128), 1)
-    sub = lax.broadcasted_iota(jnp.int32, (8, 128), 0)
-    mine = lane // 32 == sub % 4
     for r in range(0, PROWS, 2):
         out = []
         for k in (r, r + 1):
@@ -233,6 +249,7 @@
         hi, lo = _split(jnp.concatenate(out, axis=0))
         e3[24 * r:24 * r + 48, 0:128] = hi
         e3[24 * r:24 * r + 48, 128:256] = lo
+        yield 25
     for q in range(NQ):
         cur = None
         for i in range(4):
@@ -240,6 +257,13 @@
             v = _roll(fixed[row], 32 * i - pixel, 1)
             cur = v if i == 0 else jnp.where(lane < 32 * i, cur, v)
         ef[q] = cur
+        yield 25
+
+
+def _start(field, pixel, s, raw):
+    lane = lax.broadcasted_iota(jnp.int32, (8, 128), 1)
+    sub = lax.broadcasted_iota(jnp.int32, (8, 128), 0)
+    mine = lane // 32 == sub % 4
     for comp in range(2):
         for b in range(NQ // 2):
             v = field[comp][8 * b + 4:8 * b + 12]
@@ -259,11 +283,16 @@
             rows[h][8 * b + k] = v
             rows_ref[h, 8 * b + k] = v
 
-    _embed(_Place(), moving, fixed, lane, w1_ref, bias_ref, w2_ref, hs, sink)
+    blank = jnp.zeros((16, 128), jnp.float32)
+    fixed = jnp.concatenate([blank, fixed, blank], axis=0)
+    for _ in _embed(_Place(), [moving, fixed], lane, [TOP, TOP], [range(BLOCKS), FIXED_BLOCKS],
+                    w1_ref, bias_ref, w2_ref, hs, sink):
+        pass
     raw_ref[...] = jnp.zeros_like(raw_ref)
     for s in range(1, SEGS - 1):
-        _build(rows[0], rows[1], field, WIDE * s - 3 - REACH, WIDE * s - SIDE, s,
-               e3_ref.at[s - 1], ef_ref.at[s - 1], raw_ref)
+        _start(field, WIDE * s - SIDE, s, raw_ref)
+        for _ in _build(rows[0], rows[1], WIDE * s - 3 - REACH, WIDE * s - SIDE, e3_ref.at[s - 1], ef_ref.at[s - 1]):
+            pass
 
 
 def _refine(own_ref, up_ref, down_ref, one_ref, two_ref, w1_ref, bias_ref, w2_ref, mid3_ref, midf_ref, midr_ref, rows_ref,
@@ -272,22 +301,37 @@
     row0, col0, rows, cols = place.row, place.col, place.rows, place.cols
     lane = lax.broadcasted_iota(jnp.int32, (8, 128), 1)
     sub = lax.broadcasted_iota(jnp.int32, (8, 128), 0)
-    moving, fixed, *field = _strips(_own(own_ref), up_ref[...], down_ref[...], one_ref[...], two_ref[...])
-    column = jnp.where(lane < AT4, lane - FROM0, jnp.where(lane < 126, lane + FROM4, lane - 126 - HALO_M))
-    edge = [[{}, {}], [{}, {}]]
-
-    def sink(b, h, got):
-        for k, v in enumerate(got):
-            mine = rows_ref[h, 8 * b + k]
-            edge[0][h][8 * b + k] = jnp.where(lane < 30, v, _roll(mine, FROM0, 1))
-            edge[1][h][8 * b + k] = jnp.where(lane < 90, _roll(mine, -FROM4, 1), v)
-
-    _embed(place, moving, fixed, column, w1_ref, bias_ref, w2_ref, hs, sink)
+    image, *field = _edges(_own(own_ref), up_ref[...], down_ref[...], one_ref[...], two_ref[...])
     raw[...] = midr_ref[...]
-    _build(edge[0][0], edge[0][1], field, 0, REACH, 0, e3.at[0], ef.at[0], raw)
-    _build(edge[1][0], edge[1][1], field, AT4, AT4 + REACH, SEGS - 1, e3.at[1], ef.at[1], raw)
+    _start(field, REACH, 0, raw)
+    _start(field, AT4 + REACH, SEGS - 1, raw)
     tables = [e3.at[0]] + [mid3_ref.at[k] for k in range(SEGS - 2)] + [e3.at[1]]
     targets = [ef.at[0]] + [midf_ref.at[k] for k in range(SEGS - 2)] + [ef.at[1]]
+
+    def edges(ready):
+        rows = [[{}, {}], [{}, {}]]
+
+        def sink(b, h, got):
+            for k, v in enumerate(got):
+                r = 8 * (b + HALF * h) + k
+                mine = rows_ref[0, r]
+                rows[0][0][r] = jnp.where(lane < FROM0 + 2, _roll(v, FROM0 - HALO_M, 1), _roll(mine, FROM0, 1))
+                rows[1][0][r] = jnp.where(lane < TC - FROM4 - 2, _roll(mine, -FROM4, 1), _roll(v, FAR - 32 - FROM4, 1))
+                if r // 8 in FIXED_BLOCKS:
+                    mine = rows_ref[1, r]
+                    rows[0][1][r] = jnp.where(lane < FROM0 + 2, _roll(v, FROM0 - HALO_M - 64, 1), _roll(mine, FROM0, 1))
+                    rows[1][1][r] = jnp.where(lane < TC - FROM4 - 2, _roll(mine, -FROM4, 1), _roll(v, FAR - 96 - FROM4, 1))
+
+        column = jnp.where(lane % 64 < 32, lane % 32 - HALO_M, lane % 32 + FAR)
+        blank = jnp.zeros((8, 128), jnp.float32)
+        halves = [image[:8 * HALF + 16], jnp.concatenate([image[8 * HALF:], blank, blank], axis=0)]
+        yield from _embed(place, halves, column, [TOP, TOP + 8 * HALF], [range(HALF), range(BLOCKS - HALF)],
+                          w1_ref, bias_ref, w2_ref, hs, sink)
+        yield from _build(rows[0][0], rows[0][1], 0, REACH, e3.at[0], ef.at[0])
+        ready.extend((q0, 0) for q0 in range(0, NQ, 2))
+        yield from _build(rows[1][0], rows[1][1], AT4, AT4 + REACH, e3.at[1], ef.at[1])
+        ready.extend((q0, SEGS - 1) for q0 in range(0, NQ, 2))
+
     m1[...] = jnp.zeros_like(m1)
     m2[...] = jnp.zeros_like(m2)
     dat[...] = jnp.zeros_like(dat)
@@ -355,9 +399,17 @@
                 disp[comp, q] = jnp.where(ok, d, 0.0)
                 frac[comp, q] = d - n
                 idx[comp, q] = n + origin.astype(jnp.float32)
-        for q0 in range(0, NQ, 2) if t < 2 else range(1, NQ - 1, 2):
-            for s in range(SEGS):
-                group(q0, s)
+        if t == 0:
+            ready, spent = [(q0, s) for s in range(1, SEGS - 1) for q0 in range(0, NQ, 2)], 0
+            for length in edges(ready):
+                spent += length
+                while spent >= PACE and ready:
+                    spent -= PACE
+                    group(*ready.pop(0))
+        else:
+            ready = [(q0, s) for q0 in (range(0, NQ, 2) if t < 2 else range(1, NQ - 1, 2)) for s in range(SEGS)]
+        for at in ready:
+            group(*at)
         one, two = 1.0 / (1.0 - 0.9 ** (t + 1)), 1.0 / (1.0 - 0.999 ** (t + 1))
         for comp in range(2):
             for q in range(NQ) if t < 2 else range(1, NQ - 1):
@@ -388,13 +440,13 @@
             out_ref[comp, 8 * b:8 * b + 8] = out - own[2 + comp][8 * b:8 * b + 8]
 
 
-def _swaps(n, first):
-    return [p for a in range(first, n, 2) for p in ((a, (a + 1) % n), ((a + 1) % n, a))]
+def _swaps(n, first, wrap):
+    return [p for a in range(first, n if wrap else n - 1, 2) for p in ((a, (a + 1) % n), ((a + 1) % n, a))]
 
 
 def _exchange(pair, axis):
     n = lax.axis_size(axis)
-    return [lax.ppermute(x, axis, _swaps(n, k)) for k, x in enumerate(pair)]
+    return [lax.ppermute(x, axis, _swaps(n, k, axis == "row")) for k, x in enumerate(pair)]
 
 
 def _local(fixed_section, moving_section, field_init, first_weight, first_bias, second_weight):
@@ -422,7 +474,7 @@
     w1, w2, bias = call(_weights, "weights", [((128, 48), bf16), ((384, 160), bf16), ((CH, 128), f32)],
                         [anywhere, anywhere, smem], [
         pltpu.VMEM((CH, 9), f32), pltpu.VMEM((CH, CH, 9), f32), pltpu.VMEM((2, CH, 128), f32),
-        pltpu.SemaphoreType.DMA((2,))])(first_weight, second_weight, first_bias)
+        pltpu.SemaphoreType.DMA((2,))])(*[pltpu.with_memory_space_constraint(x, pltpu.HBM) for x in (first_weight, second_weight)], first_bias)
     strip = ((TALL, 128), f32)
     one, two = _exchange(call(_pack_cols, "pack_cols", [strip, strip], [vmem] * 4, [])(own, up, down, bias), "col")
     hidden = pltpu.VMEM((2, HROWS * CH, 256), bf16)

time: 22.9 us -> 21.8 us (0.952)
  the two profiles are of different devices: /device:TPU:0 before, /device:TPU:1 now
where the time goes in v3:
time: 21.8 us; the launch traced here: 21.6 us
  Pallas kernels  11.8 us (54%)
  starting transfers between devices  8.35 us (38%)
  waiting for transfers between devices  0.74 us (3%)
  local copies, waits for them, and re-layouts  0.65 us (3%)
    ppermute x4, starting transfers between devices, _exchange(): lax.ppermute(x, axis, _swaps(n, k, axis == 'row'))  8.35 us
    pallas_call x1, Pallas kernels, _local(): call(_refine, 'refine', [((2, TR, TC), f32)], [vmem] * 12, [hidden, pltpu...  7.45 us
    pallas_call x1, Pallas kernels, _local(): call(_middle, 'middle', [((SEGS - 2,) + table, bf16), ((SEGS - 2,) + targ...  1.76 us
    pallas_call x1, Pallas kernels, _local(): call(_weights, 'weights', [((128, 48), bf16), ((384, 160), bf16), ((CH, 1...  1.62 us
    pallas_call x1, Pallas kernels, _local(): call(_pack_rows, 'pack_rows', [strip, strip, ((4 * TR, TC), f32)], [anywh...  0.83 us
    ppermute x4, waiting for transfers between devices, _exchange(): lax.ppermute(x, axis, _swaps(n, k, axis == 'row'))  0.74 us
    unnamed x2, local copies, waits for them, and re-layouts  0.65 us
  transfers between devices with their start and end apart: 4, of which 2 were waited for; matrix products, arithmetic and copies ran while one was open for 0% of the time, Pallas kernels for 16%

profile of v3, /device:TPU:1, one launch (start us, length us, event | category | flops | bytes accessed | tf_op | source)
XLA Modules:
  0.0 21.6 jit_solution(16950789223612968925)
XLA Ops:
  0.0 0.8 %pack_rows.1 = (f32[48,128]{1,0:T(8,128)S(1)}, f32[48,128]{1,0:T(8,128)S(1)}, f32[128,128]{1,0:T(8,128)S(1)}) custom-call(bf16[32,128]{1,0:T(8,128)(2,1)} %mv_ref.1, bf16[32,128]{1,0:T(8,128)(2,1)} %fx_ref.1, f32[2,32,128]{2,1,0:T(8,128)} %fd_ref.1), custom_call_target="tpu_custom_call" | custom-call | tf_op jit(solution)/shard_map/pack_rows/pallas_call | solution.py:470
  0.8 2.1 %collective-permute-start = (f32[48,128]{1,0:T(8,128)S(1)}, f32[48,128]{1,0:T(8,128)S(1)}, u32[]{:S(2)}, u32[]{:S(2)}) collective-permute-start(f32[48,128]{1,0:T(8,128)S(1)} %get-tuple-element.18), channel_id=1, source_target_pairs={{0,8},{8,0},{16,24},{24,16},{1,9},{9,1},{17,25},{25,17},{2,10},{10... | collective-permute-start | bytes 73736 | tf_op jit(solution)/shard_map/ppermute | solution.py:449
  2.9 1.2 %collective-permute-start.1 = (f32[48,128]{1,0:T(8,128)S(1)}, f32[48,128]{1,0:T(8,128)S(1)}, u32[]{:S(2)}, u32[]{:S(2)}) collective-permute-start(f32[48,128]{1,0:T(8,128)S(1)} %get-tuple-element.19), channel_id=1, source_target_pairs={{8,16},{16,8},{24,0},{0,24},{9,17},{17,9},{25,1},{1,25},{10,18},{1... | collective-permute-start | bytes 73736 | tf_op jit(solution)/shard_map/ppermute | solution.py:449
  4.2 0.0 copy-start
  4.2 0.7 %copy-done = f32[8]{0:T(128)S(1)} copy-done((f32[8]{0:T(128)S(1)}, f32[8]{0:T(128)}, u32[]{:S(2)}) %copy-start) | copy-done | bytes 56
  4.8 1.6 %weights.1 = (bf16[128,48]{1,0:T(8,128)(2,1)S(1)}, bf16[384,160]{1,0:T(8,128)(2,1)S(1)}, f32[8,128]{1,0:T(8,128)S(1)}) custom-call(f32[8,9]{1,0:T(8,128)} %w1_ref.1, f32[8,8,9]{2,1,0:T(8,128)} %w2_ref.1, f32[8]{0:T(128)S(1)} %copy-done), custom_call_target="tpu_custom_call" | custom-call | tf_op jit(solution)/shard_map/weights/pallas_call | solution.py:474
  6.4 0.0 collective-permute-done.up_ref
  6.4 0.3 %collective-permute-done.1.down_ref = f32[48,128]{1,0:T(8,128)S(1)} collective-permute-done((f32[48,128]{1,0:T(8,128)S(1)}, f32[48,128]{1,0:T(8,128)S(1)}, u32[]{:S(2)}, u32[]{:S(2)}) %collective-permute-start.1) | collective-permute-done | bytes 24608 | tf_op jit(solution)/shard_map/ppermute | solution.py:449
  6.8 0.1 pack_cols.1
  6.9 1.9 %collective-permute-start.2 = (f32[80,128]{1,0:T(8,128)S(1)}, f32[80,128]{1,0:T(8,128)S(1)}, u32[]{:S(2)}, u32[]{:S(2)}) collective-permute-start(f32[80,128]{1,0:T(8,128)S(1)} %get-tuple-element.21), channel_id=1, source_target_pairs={{0,1},{1,0},{2,3},{3,2},{4,5},{5,4},{6,7},{7,6},{8,9},{9,8},{10,11... | collective-permute-start | bytes 122888 | tf_op jit(solution)/shard_map/ppermute | solution.py:449
  8.8 3.1 %collective-permute-start.3 = (f32[80,128]{1,0:T(8,128)S(1)}, f32[80,128]{1,0:T(8,128)S(1)}, u32[]{:S(2)}, u32[]{:S(2)}) collective-permute-start(f32[80,128]{1,0:T(8,128)S(1)} %get-tuple-element.22), channel_id=1, source_target_pairs={{1,2},{2,1},{3,4},{4,3},{5,6},{6,5},{9,10},{10,9},{11,12},{12,11},... | collective-permute-start | bytes 122888 | tf_op jit(solution)/shard_map/ppermute | solution.py:449
  11.9 1.8 %middle.1 = (bf16[3,1248,256]{2,1,0:T(8,128)(2,1)S(1)}, f32[3,10,8,128]{3,2,1,0:T(8,128)S(1)}, f32[2,10,8,128]{3,2,1,0:T(8,128)S(1)}, f32[2,72,8,128]{3,2,1,0:T(8,128)S(1)}) custom-call(f32[128,128]{1,0:T(8,128)S(1)} %get-tuple-element.17.own_ref, f32[48,128]{1,0:T(8,128)S(1)} %collective-permute-done.up_ref, f32[48,128]{1,0:T(8,128)S(1)} %collective-permute-done.1.down_ref, ...), custom_call_target="tpu_custom_call" | custom-call | tf_op jit(solution)/shard_map/middle/pallas_call | solution.py:482
  13.7 0.0 collective-permute-done.2.one_ref
  13.7 0.4 %collective-permute-done.3.two_ref = f32[80,128]{1,0:T(8,128)S(1)} collective-permute-done((f32[80,128]{1,0:T(8,128)S(1)}, f32[80,128]{1,0:T(8,128)S(1)}, u32[]{:S(2)}, u32[]{:S(2)}) %collective-permute-start.3) | collective-permute-done | bytes 40992 | tf_op jit(solution)/shard_map/ppermute | solution.py:449
  14.1 7.5 %refine.1 = f32[2,32,128]{2,1,0:T(8,128)} custom-call(f32[128,128]{1,0:T(8,128)S(1)} %get-tuple-element.17.own_ref, f32[48,128]{1,0:T(8,128)S(1)} %collective-permute-done.up_ref, f32[48,128]{1,0:T(8,128)S(1)} %collective-permute-done.1.down_ref, f32[80,128]{1,0:T(8,128)S(1)} %collective-permute-done.2.one_ref, ...), custom_call_target="tpu_custom_call" | custom-call | tf_op jit(solution)/shard_map/refine/pallas_call | solution.py:485
Async XLA Ops:
  0.8 5.6 %collective-permute-start = (f32[48,128]{1,0:T(8,128)S(1)}, f32[48,128]{1,0:T(8,128)S(1)}, u32[]{:S(2)}, u32[]{:S(2)}) collective-permute-start(f32[48,128]{1,0:T(8,128)S(1)} %get-tuple-element.18), channel_id=1, source_target_pairs={{0,8},{8,0},{16,24},{24,16},{1,9},{9,1},{17,25},{25,17},{2,10},{10... | collective-permute-start | bytes 73736 | tf_op jit(solution)/shard_map/ppermute | solution.py:449
  2.9 3.8 %collective-permute-start.1 = (f32[48,128]{1,0:T(8,128)S(1)}, f32[48,128]{1,0:T(8,128)S(1)}, u32[]{:S(2)}, u32[]{:S(2)}) collective-permute-start(f32[48,128]{1,0:T(8,128)S(1)} %get-tuple-element.19), channel_id=1, source_target_pairs={{8,16},{16,8},{24,0},{0,24},{9,17},{17,9},{25,1},{1,25},{10,18},{1... | collective-permute-start | bytes 73736 | tf_op jit(solution)/shard_map/ppermute | solution.py:449
  4.2 0.7 %copy-start = (f32[8]{0:T(128)S(1)}, f32[8]{0:T(128)}, u32[]{:S(2)}) copy-start(f32[8]{0:T(128)} %bias_ref.1) | copy-start | bytes 100
  6.9 6.8 %collective-permute-start.2 = (f32[80,128]{1,0:T(8,128)S(1)}, f32[80,128]{1,0:T(8,128)S(1)}, u32[]{:S(2)}, u32[]{:S(2)}) collective-permute-start(f32[80,128]{1,0:T(8,128)S(1)} %get-tuple-element.21), channel_id=1, source_target_pairs={{0,1},{1,0},{2,3},{3,2},{4,5},{5,4},{6,7},{7,6},{8,9},{9,8},{10,11... | collective-permute-start | bytes 122888 | tf_op jit(solution)/shard_map/ppermute | solution.py:449
  8.8 5.3 %collective-permute-start.3 = (f32[80,128]{1,0:T(8,128)S(1)}, f32[80,128]{1,0:T(8,128)S(1)}, u32[]{:S(2)}, u32[]{:S(2)}) collective-permute-start(f32[80,128]{1,0:T(8,128)S(1)} %get-tuple-element.22), channel_id=1, source_target_pairs={{1,2},{2,1},{3,4},{4,3},{5,6},{6,5},{9,10},{10,9},{11,12},{12,11},... | collective-permute-start | bytes 122888 | tf_op jit(solution)/shard_map/ppermute | solution.py:449

commit v4 on v3

--- a/solution.py
+++ b/solution.py
@@ -18,6 +18,8 @@
 HALO_PAD = 24
 PADS = (HALO_PAD, 8, 8, 8)
 TALL = TR + 2 * HALO_PAD
+WIDTHS = (HALO_M, 4, SIDE, SIDE)
+STRIPS = (0, HALO_M, HALO_M + 4, HALO_M + 4 + SIDE)
 EROWS = 72
 HROWS = 80
 TOP = -(REACH + 3)
@@ -33,7 +35,7 @@
 
 FROM0 = REACH + 3
 FAR = 117
-PACE = 600
+PACE = 300
 HALF = 5
 AT4 = 62
 FROM4 = WIDE * (SEGS - 1) - FROM0 - AT4
@@ -152,31 +154,35 @@
     even = lax.rem(lax.axis_index("col"), 2) == 0
     tall = _tall(_own(own_ref), up_ref[...], down_ref[...])
     lane = lax.broadcasted_iota(jnp.int32, (8, 128), 1)
-    for i in range(TALL // 8):
-        first = last = None
-        for k in (3, 2, 1, 0):
-            if 8 * i < tall[k].shape[0]:
-                v = tall[k][8 * i:8 * i + 8]
-                a, b = _roll(v, 32 * k, 1), _roll(v, 32 * k + HALO_M, 1)
-                first = a if first is None else jnp.where(lane < 32 * k + 32, a, first)
-                last = b if last is None else jnp.where(lane < 32 * k + 32, b, last)
-        one_ref[8 * i:8 * i + 8] = jnp.where(even, last, first)
-        two_ref[8 * i:8 * i + 8] = jnp.where(even, first, last)
+    for i in range(0, TALL // 8, 4):
+        first = last = jnp.zeros((8, 128), jnp.float32)
+        for b in range(i, min(i + 4, TALL // 8)):
+            for k, x in enumerate(tall):
+                if 8 * b < x.shape[0]:
+                    v, at = x[8 * b:8 * b + 8], 32 * (b - i) + STRIPS[k]
+                    first = jnp.where(lane < at, first, _roll(v, at, 1))
+                    last = jnp.where(lane < at, last, _roll(v, at + WIDTHS[k], 1))
+        one_ref[2 * i:2 * i + 8] = jnp.where(even, last, first)
+        two_ref[2 * i:2 * i + 8] = jnp.where(even, first, last)
+
+
+def _unpack(x):
+    return jnp.concatenate([_roll(x[8 * (b // 4):8 * (b // 4) + 8], -32 * (b % 4), 1) for b in range(TALL // 8)], axis=0)
 
 
 def _edges(own, up, down, one, two):
     c, n = lax.axis_index("col"), lax.axis_size("col")
     even = lax.rem(c, 2) == 0
-    left = jnp.where(c > 0, jnp.where(even, two, one), 0.0)
-    right = jnp.where(c < n - 1, jnp.where(even, one, two), 0.0)
+    left = _unpack(jnp.where(c > 0, jnp.where(even, two, one), 0.0))
+    right = _unpack(jnp.where(c < n - 1, jnp.where(even, one, two), 0.0))
     tall = _tall(own, up, down)
     images = []
     for k, x in enumerate(tall[:2]):
         lane = lax.broadcasted_iota(jnp.int32, x.shape, 1) - 64 * k
         r = x.shape[0]
-        v = jnp.where(lane < 32 + TC - FAR, _roll(x, 64 * k + 32 - FAR, 1), _roll(right[:r], 32 * k + 32 + TC - FAR, 1))
+        v = jnp.where(lane < 32 + TC - FAR, _roll(x, 64 * k + 32 - FAR, 1), _roll(right[:r], 64 * k + 32 + TC - FAR - STRIPS[k], 1))
         v = jnp.where(lane < 32, _roll(x, 64 * k + HALO_M, 1), v)
-        images.append(jnp.where(lane < HALO_M, _roll(left[:r], 32 * k, 1), v))
+        images.append(jnp.where(lane < HALO_M, _roll(left[:r], 64 * k + HALO_M - WIDTHS[k] - STRIPS[k], 1), v))
     blank = jnp.zeros((16, 128), jnp.float32)
     fixed = jnp.concatenate([blank, images[1], blank], axis=0)
     lane = lax.broadcasted_iota(jnp.int32, fixed.shape, 1)
@@ -185,9 +191,9 @@
         x = tall[k]
         lane = lax.broadcasted_iota(jnp.int32, x.shape, 1)
         r = x.shape[0]
-        v = jnp.where(lane < TC - FROM4, _roll(x, -FROM4, 1), _roll(right[:r], TC - FROM4 - 32 * k, 1))
+        v = jnp.where(lane < TC - FROM4, _roll(x, -FROM4, 1), _roll(right[:r], TC - FROM4 - STRIPS[k], 1))
         v = jnp.where(lane < AT4, _roll(x, FROM0, 1), v)
-        out.append(jnp.where(lane < FROM0, _roll(left[:r], FROM0 - HALO_M - 32 * k, 1), v))
+        out.append(jnp.where(lane < FROM0, _roll(left[:r], FROM0 - WIDTHS[k] - STRIPS[k], 1), v))
     return out
 
 
@@ -223,7 +229,7 @@
                 jnp.maximum(pre[CH * k:CH * k + CH, at] + bias, 0.0) * place.keep(tops[h] - 1 + 8 * b + k, col_ok)
                 for k in range(8)], axis=0)
             hs[0, 64 * b:64 * b + 64, at], hs[1, 64 * b:64 * b + 64, at] = _split(v)
-        yield 200
+        yield 100
     for b in range(count):
         t = _dot(w2_ref[...], jnp.concatenate([hs[0, 64 * b:64 * b + 80], hs[1, 64 * b:64 * b + 80]], axis=0))
         v = t[:192] + t[192:]
@@ -233,7 +239,7 @@
             o = [v[64 * kx:64 * kx + 64, 128 * h:128 * h + 128] for kx in range(3)]
             e = o[1] + _roll(o[0], 1, 1) + _roll(o[2], -1, 1)
             sink(b, h, [e[CH * k:CH * k + CH] * place.keep(tops[h] + 8 * b + k, col_ok) for k in range(8)])
-        yield 250
+        yield 120
 
 
 def _build(moving, fixed, window, pixel, e3, ef):
@@ -332,8 +338,6 @@
         yield from _build(rows[1][0], rows[1][1], AT4, AT4 + REACH, e3.at[1], ef.at[1])
         ready.extend((q0, SEGS - 1) for q0 in range(0, NQ, 2))
 
-    m1[...] = jnp.zeros_like(m1)
-    m2[...] = jnp.zeros_like(m2)
     dat[...] = jnp.zeros_like(dat)
 
     j = lane % 32
@@ -406,38 +410,46 @@
                 while spent >= PACE and ready:
                     spent -= PACE
                     group(*ready.pop(0))
-        else:
-            ready = [(q0, s) for q0 in (range(0, NQ, 2) if t < 2 else range(1, NQ - 1, 2)) for s in range(SEGS)]
-        for at in ready:
-            group(*at)
+            for at in ready:
+                group(*at)
+        for q0 in range(0, NQ, 2) if t < 2 else range(1, NQ - 1, 2):
+            if t > 0:
+                for s in range(SEGS):
+                    group(q0, s)
+            for comp in range(2):
+                for q in (q0, q0 + 1):
+                    update(t, comp, q)
+                if t == 2:
+                    finish(comp, q0 // 2)
+
+    def update(t, comp, q):
         one, two = 1.0 / (1.0 - 0.9 ** (t + 1)), 1.0 / (1.0 - 0.999 ** (t + 1))
-        for comp in range(2):
-            for q in range(NQ) if t < 2 else range(1, NQ - 1):
-                d = disp[comp, q]
-                up = jnp.where(lane < 96, _roll(d, -32, 1), _roll(disp[comp, min(q + 1, NQ - 1)], -32, 1))
-                down = jnp.where(lane >= 32, _roll(d, 32, 1), _roll(disp[comp, max(q - 1, 0)], 32, 1))
-                around = up + down + _roll(d, 1, 1) + _roll(d, -1, 1)
-                v = sq[comp, q]
-                grad = (dat[comp, q] + 2.0 * STIFFNESS * (4.0 * REACH * v - around)) * (1.0 - v * v)
-                a = 0.9 * m1[comp, q] + 0.1 * grad
-                b = 0.999 * m2[comp, q] + 0.001 * grad * grad
-                m1[comp, q] = a
-                m2[comp, q] = b
-                raw[comp, q] = raw[comp, q] - STEP * (a * one) / (jnp.sqrt(b * two) + EPS)
+        d = disp[comp, q]
+        up = jnp.where(lane < 96, _roll(d, -32, 1), _roll(disp[comp, min(q + 1, NQ - 1)], -32, 1))
+        down = jnp.where(lane >= 32, _roll(d, 32, 1), _roll(disp[comp, max(q - 1, 0)], 32, 1))
+        around = up + down + _roll(d, 1, 1) + _roll(d, -1, 1)
+        v = sq[comp, q]
+        grad = (dat[comp, q] + 2.0 * STIFFNESS * (4.0 * REACH * v - around)) * (1.0 - v * v)
+        a, b = 0.1 * grad, 0.001 * grad * grad
+        if t > 0:
+            a, b = 0.9 * m1[comp, q] + a, 0.999 * m2[comp, q] + b
+        m1[comp, q] = a
+        m2[comp, q] = b
+        raw[comp, q] = raw[comp, q] - STEP * (a * one) / (jnp.sqrt(b * two) + EPS)
+
+    own = _own(own_ref)
+
+    def finish(comp, b):
+        out = None
+        for s in range(SEGS):
+            v = jnp.where(sub < 4, jnp.broadcast_to(raw[comp, 2 * b + 1, s:s + 1, :], (8, 128)),
+                          jnp.broadcast_to(raw[comp, 2 * b + 2, s:s + 1, :], (8, 128)))
+            v = _pick(v, (lane + 32 * (sub % 4) + (128 + SIDE - WIDE * s)) & 127)
+            out = v if s == 0 else jnp.where(lane < WIDE * s, out, v)
+        out_ref[comp, 8 * b:8 * b + 8] = out - own[2 + comp][8 * b:8 * b + 8]
 
     for t in range(ITERS):
         step(t)
-
-    own = _own(own_ref)
-    for comp in range(2):
-        for b in range(TR // 8):
-            out = None
-            for s in range(SEGS):
-                v = jnp.where(sub < 4, jnp.broadcast_to(raw[comp, 2 * b + 1, s:s + 1, :], (8, 128)),
-                              jnp.broadcast_to(raw[comp, 2 * b + 2, s:s + 1, :], (8, 128)))
-                v = _pick(v, (lane + 32 * (sub % 4) + (128 + SIDE - WIDE * s)) & 127)
-                out = v if s == 0 else jnp.where(lane < WIDE * s, out, v)
-            out_ref[comp, 8 * b:8 * b + 8] = out - own[2 + comp][8 * b:8 * b + 8]
 
 
 def _swaps(n, first, wrap):
@@ -475,7 +487,7 @@
                         [anywhere, anywhere, smem], [
         pltpu.VMEM((CH, 9), f32), pltpu.VMEM((CH, CH, 9), f32), pltpu.VMEM((2, CH, 128), f32),
         pltpu.SemaphoreType.DMA((2,))])(*[pltpu.with_memory_space_constraint(x, pltpu.HBM) for x in (first_weight, second_weight)], first_bias)
-    strip = ((TALL, 128), f32)
+    strip = ((8 * pl.cdiv(TALL, 32), 128), f32)
     one, two = _exchange(call(_pack_cols, "pack_cols", [strip, strip], [vmem] * 4, [])(own, up, down, bias), "col")
     hidden = pltpu.VMEM((2, HROWS * CH, 256), bf16)
     table, target = (PROWS * 24, 256), (NQ, CH, 128)

time: 21.8 us -> 21.5 us (0.986)
  waiting for transfers between devices: 0.74 us -> 0.44 us
    ppermute x4, waiting for transfers between devices: 0.74 us -> 0.44 us  [_exchange(): lax.ppermute(x, axis, _swaps(n, k, axis == 'row'))]
where the time goes in v4:
time: 21.5 us; the launch traced here: 21.3 us
  Pallas kernels  11.8 us (55%)
  starting transfers between devices  8.35 us (39%)
  local copies, waits for them, and re-layouts  0.65 us (3%)
  waiting for transfers between devices  0.44 us (2%)
    ppermute x4, starting transfers between devices, _exchange(): lax.ppermute(x, axis, _swaps(n, k, axis == 'row'))  8.35 us
    pallas_call x1, Pallas kernels, _local(): call(_refine, 'refine', [((2, TR, TC), f32)], [vmem] * 12, [hidden, pltpu...  7.47 us
    pallas_call x1, Pallas kernels, _local(): call(_middle, 'middle', [((SEGS - 2,) + table, bf16), ((SEGS - 2,) + targ...  1.76 us
    pallas_call x1, Pallas kernels, _local(): call(_weights, 'weights', [((128, 48), bf16), ((384, 160), bf16), ((CH, 1...  1.62 us
    pallas_call x1, Pallas kernels, _local(): call(_pack_rows, 'pack_rows', [strip, strip, ((4 * TR, TC), f32)], [anywh...  0.83 us
    unnamed x2, local copies, waits for them, and re-layouts  0.65 us
    ppermute x4, waiting for transfers between devices, _exchange(): lax.ppermute(x, axis, _swaps(n, k, axis == 'row'))  0.44 us
  transfers between devices with their start and end apart: 4, of which 2 were waited for; matrix products, arithmetic and copies ran while one was open for 0% of the time, Pallas kernels for 16%

profile of v4, /device:TPU:1, one launch (start us, length us, event | category | flops | bytes accessed | tf_op | source)
XLA Modules:
  0.0 21.3 jit_solution(3795098693246978435)
XLA Ops:
  0.0 0.8 %pack_rows.1 = (f32[48,128]{1,0:T(8,128)S(1)}, f32[48,128]{1,0:T(8,128)S(1)}, f32[128,128]{1,0:T(8,128)S(1)}) custom-call(bf16[32,128]{1,0:T(8,128)(2,1)} %mv_ref.1, bf16[32,128]{1,0:T(8,128)(2,1)} %fx_ref.1, f32[2,32,128]{2,1,0:T(8,128)} %fd_ref.1), custom_call_target="tpu_custom_call" | custom-call | tf_op jit(solution)/shard_map/pack_rows/pallas_call | solution.py:482
  0.8 2.1 %collective-permute-start = (f32[48,128]{1,0:T(8,128)S(1)}, f32[48,128]{1,0:T(8,128)S(1)}, u32[]{:S(2)}, u32[]{:S(2)}) collective-permute-start(f32[48,128]{1,0:T(8,128)S(1)} %get-tuple-element.18), channel_id=1, source_target_pairs={{0,8},{8,0},{16,24},{24,16},{1,9},{9,1},{17,25},{25,17},{2,10},{10... | collective-permute-start | bytes 73736 | tf_op jit(solution)/shard_map/ppermute | solution.py:461
  2.9 1.2 %collective-permute-start.1 = (f32[48,128]{1,0:T(8,128)S(1)}, f32[48,128]{1,0:T(8,128)S(1)}, u32[]{:S(2)}, u32[]{:S(2)}) collective-permute-start(f32[48,128]{1,0:T(8,128)S(1)} %get-tuple-element.19), channel_id=1, source_target_pairs={{8,16},{16,8},{24,0},{0,24},{9,17},{17,9},{25,1},{1,25},{10,18},{1... | collective-permute-start | bytes 73736 | tf_op jit(solution)/shard_map/ppermute | solution.py:461
  4.2 0.0 copy-start
  4.2 0.7 %copy-done = f32[8]{0:T(128)S(1)} copy-done((f32[8]{0:T(128)S(1)}, f32[8]{0:T(128)}, u32[]{:S(2)}) %copy-start) | copy-done | bytes 56
  4.8 1.6 %weights.1 = (bf16[128,48]{1,0:T(8,128)(2,1)S(1)}, bf16[384,160]{1,0:T(8,128)(2,1)S(1)}, f32[8,128]{1,0:T(8,128)S(1)}) custom-call(f32[8,9]{1,0:T(8,128)} %w1_ref.1, f32[8,8,9]{2,1,0:T(8,128)} %w2_ref.1, f32[8]{0:T(128)S(1)} %copy-done), custom_call_target="tpu_custom_call" | custom-call | tf_op jit(solution)/shard_map/weights/pallas_call | solution.py:486
  6.4 0.0 collective-permute-done.up_ref
  6.4 0.3 %collective-permute-done.1.down_ref = f32[48,128]{1,0:T(8,128)S(1)} collective-permute-done((f32[48,128]{1,0:T(8,128)S(1)}, f32[48,128]{1,0:T(8,128)S(1)}, u32[]{:S(2)}, u32[]{:S(2)}) %collective-permute-start.1) | collective-permute-done | bytes 24608 | tf_op jit(solution)/shard_map/ppermute | solution.py:461
  6.8 0.1 pack_cols.1
  6.9 1.9 %collective-permute-start.2 = (f32[24,128]{1,0:T(8,128)S(1)}, f32[24,128]{1,0:T(8,128)S(1)}, u32[]{:S(2)}, u32[]{:S(2)}) collective-permute-start(f32[24,128]{1,0:T(8,128)S(1)} %get-tuple-element.21), channel_id=1, source_target_pairs={{0,1},{1,0},{2,3},{3,2},{4,5},{5,4},{6,7},{7,6},{8,9},{9,8},{10,11... | collective-permute-start | bytes 36872 | tf_op jit(solution)/shard_map/ppermute | solution.py:461
  8.8 3.1 %collective-permute-start.3 = (f32[24,128]{1,0:T(8,128)S(1)}, f32[24,128]{1,0:T(8,128)S(1)}, u32[]{:S(2)}, u32[]{:S(2)}) collective-permute-start(f32[24,128]{1,0:T(8,128)S(1)} %get-tuple-element.22), channel_id=1, source_target_pairs={{1,2},{2,1},{3,4},{4,3},{5,6},{6,5},{9,10},{10,9},{11,12},{12,11},... | collective-permute-start | bytes 36872 | tf_op jit(solution)/shard_map/ppermute | solution.py:461
  11.9 1.8 %middle.1 = (bf16[3,1248,256]{2,1,0:T(8,128)(2,1)S(1)}, f32[3,10,8,128]{3,2,1,0:T(8,128)S(1)}, f32[2,10,8,128]{3,2,1,0:T(8,128)S(1)}, f32[2,72,8,128]{3,2,1,0:T(8,128)S(1)}) custom-call(f32[128,128]{1,0:T(8,128)S(1)} %get-tuple-element.17.own_ref, f32[48,128]{1,0:T(8,128)S(1)} %collective-permute-done.up_ref, f32[48,128]{1,0:T(8,128)S(1)} %collective-permute-done.1.down_ref, ...), custom_call_target="tpu_custom_call" | custom-call | tf_op jit(solution)/shard_map/middle/pallas_call | solution.py:494
  13.7 0.0 collective-permute-done.2.one_ref
  13.7 0.1 collective-permute-done.3.two_ref
  13.8 7.5 %refine.1 = f32[2,32,128]{2,1,0:T(8,128)} custom-call(f32[128,128]{1,0:T(8,128)S(1)} %get-tuple-element.17.own_ref, f32[48,128]{1,0:T(8,128)S(1)} %collective-permute-done.up_ref, f32[48,128]{1,0:T(8,128)S(1)} %collective-permute-done.1.down_ref, f32[24,128]{1,0:T(8,128)S(1)} %collective-permute-done.2.one_ref, ...), custom_call_target="tpu_custom_call" | custom-call | tf_op jit(solution)/shard_map/refine/pallas_call | solution.py:497
Async XLA Ops:
  0.8 5.6 %collective-permute-start = (f32[48,128]{1,0:T(8,128)S(1)}, f32[48,128]{1,0:T(8,128)S(1)}, u32[]{:S(2)}, u32[]{:S(2)}) collective-permute-start(f32[48,128]{1,0:T(8,128)S(1)} %get-tuple-element.18), channel_id=1, source_target_pairs={{0,8},{8,0},{16,24},{24,16},{1,9},{9,1},{17,25},{25,17},{2,10},{10... | collective-permute-start | bytes 73736 | tf_op jit(solution)/shard_map/ppermute | solution.py:461
  2.9 3.8 %collective-permute-start.1 = (f32[48,128]{1,0:T(8,128)S(1)}, f32[48,128]{1,0:T(8,128)S(1)}, u32[]{:S(2)}, u32[]{:S(2)}) collective-permute-start(f32[48,128]{1,0:T(8,128)S(1)} %get-tuple-element.19), channel_id=1, source_target_pairs={{8,16},{16,8},{24,0},{0,24},{9,17},{17,9},{25,1},{1,25},{10,18},{1... | collective-permute-start | bytes 73736 | tf_op jit(solution)/shard_map/ppermute | solution.py:461
  4.2 0.7 %copy-start = (f32[8]{0:T(128)S(1)}, f32[8]{0:T(128)}, u32[]{:S(2)}) copy-start(f32[8]{0:T(128)} %bias_ref.1) | copy-start | bytes 100
  6.9 6.8 %collective-permute-start.2 = (f32[24,128]{1,0:T(8,128)S(1)}, f32[24,128]{1,0:T(8,128)S(1)}, u32[]{:S(2)}, u32[]{:S(2)}) collective-permute-start(f32[24,128]{1,0:T(8,128)S(1)} %get-tuple-element.21), channel_id=1, source_target_pairs={{0,1},{1,0},{2,3},{3,2},{4,5},{5,4},{6,7},{7,6},{8,9},{9,8},{10,11... | collective-permute-start | bytes 36872 | tf_op jit(solution)/shard_map/ppermute | solution.py:461
  8.8 5.0 %collective-permute-start.3 = (f32[24,128]{1,0:T(8,128)S(1)}, f32[24,128]{1,0:T(8,128)S(1)}, u32[]{:S(2)}, u32[]{:S(2)}) collective-permute-start(f32[24,128]{1,0:T(8,128)S(1)} %get-tuple-element.22), channel_id=1, source_target_pairs={{1,2},{2,1},{3,4},{4,3},{5,6},{6,5},{9,10},{10,9},{11,12},{12,11},... | collective-permute-start | bytes 36872 | tf_op jit(solution)/shard_map/ppermute | solution.py:461

commit v5 on v4

--- a/solution.py
+++ b/solution.py
@@ -150,7 +150,7 @@
     m2_ref[...] = jnp.concatenate(hi_rows + lo_rows, axis=0)[:, :160].astype(jnp.bfloat16)
 
 
-def _pack_cols(own_ref, up_ref, down_ref, _, one_ref, two_ref):
+def _pack_cols(own_ref, down_ref, up_ref, _, one_ref, two_ref):
     even = lax.rem(lax.axis_index("col"), 2) == 0
     tall = _tall(_own(own_ref), up_ref[...], down_ref[...])
     lane = lax.broadcasted_iota(jnp.int32, (8, 128), 1)
@@ -279,7 +279,7 @@
                     jnp.where(mine & (sub // 4 == k), v, 0.0), axis=0, keepdims=True)
 
 
-def _middle(own_ref, up_ref, down_ref, w1_ref, bias_ref, w2_ref, e3_ref, ef_ref, raw_ref, rows_ref, hs):
+def _middle(own_ref, down_ref, up_ref, w1_ref, bias_ref, w2_ref, e3_ref, ef_ref, raw_ref, rows_ref, hs):
     moving, fixed, *field = _tall(_own(own_ref), up_ref[...], down_ref[...])
     lane = lax.broadcasted_iota(jnp.int32, (CH, 128), 1)
     rows = [{}, {}]
@@ -301,7 +301,7 @@
             pass
 
 
-def _refine(own_ref, up_ref, down_ref, one_ref, two_ref, w1_ref, bias_ref, w2_ref, mid3_ref, midf_ref, midr_ref, rows_ref,
+def _refine(own_ref, down_ref, up_ref, one_ref, two_ref, w1_ref, bias_ref, w2_ref, mid3_ref, midf_ref, midr_ref, rows_ref,
             out_ref, hs, e3, ef, raw, m1, m2, sq, disp, frac, idx, dat):
     place = _Place()
     row0, col0, rows, cols = place.row, place.col, place.rows, place.cols
@@ -452,13 +452,26 @@
         step(t)
 
 
-def _swaps(n, first, wrap):
-    return [p for a in range(first, n if wrap else n - 1, 2) for p in ((a, (a + 1) % n), ((a + 1) % n, a))]
+def _swaps(axis, first):
+    rows, cols = lax.axis_size("row"), lax.axis_size("col")
+    n = rows if axis == "row" else cols
+    out = []
+    for r in range(rows):
+        for c in range(cols):
+            i = r if axis == "row" else c
+            j = i + 1 if (i - first) % 2 == 0 else i - 1
+            if 0 <= j < n:
+                r2, c2 = (j, c) if axis == "row" else (r, j)
+            elif axis == "row":
+                r2, c2 = r, c ^ 1
+            else:
+                r2, c2 = r ^ 1, c
+            out.append((r * cols + c, r2 * cols + c2))
+    return out
 
 
 def _exchange(pair, axis):
-    n = lax.axis_size(axis)
-    return [lax.ppermute(x, axis, _swaps(n, k, axis == "row")) for k, x in enumerate(pair)]
+    return [lax.ppermute(x, ("row", "col"), _swaps(axis, k)) for k, x in enumerate(pair)]
 
 
 def _local(fixed_section, moving_section, field_init, first_weight, first_bias, second_weight):
@@ -488,16 +501,16 @@
         pltpu.VMEM((CH, 9), f32), pltpu.VMEM((CH, CH, 9), f32), pltpu.VMEM((2, CH, 128), f32),
         pltpu.SemaphoreType.DMA((2,))])(*[pltpu.with_memory_space_constraint(x, pltpu.HBM) for x in (first_weight, second_weight)], first_bias)
     strip = ((8 * pl.cdiv(TALL, 32), 128), f32)
-    one, two = _exchange(call(_pack_cols, "pack_cols", [strip, strip], [vmem] * 4, [])(own, up, down, bias), "col")
+    one, two = _exchange(call(_pack_cols, "pack_cols", [strip, strip], [vmem] * 4, [])(own, down, up, bias), "col")
     hidden = pltpu.VMEM((2, HROWS * CH, 256), bf16)
     table, target = (PROWS * 24, 256), (NQ, CH, 128)
     mid = call(_middle, "middle", [
         ((SEGS - 2,) + table, bf16), ((SEGS - 2,) + target, f32), ((2, NQ, 8, 128), f32), ((2, EROWS, CH, 128), f32),
-    ], [vmem] * 6, [hidden])(own, up, down, w1, bias, w2)
+    ], [vmem] * 6, [hidden])(own, down, up, w1, bias, w2)
     return call(_refine, "refine", [((2, TR, TC), f32)], [vmem] * 12, [
         hidden, pltpu.VMEM((2,) + table, bf16), pltpu.VMEM((2,) + target, f32),
         *[pltpu.VMEM((2, NQ, 8, 128), f32) for _ in range(8)],
-    ])(own, up, down, one, two, w1, bias, w2, *mid)[0]
+    ])(own, down, up, one, two, w1, bias, w2, *mid)[0]
 
 
 def solution(mesh):

time: 21.5 us -> 19.3 us (0.90)
  the two profiles are of different devices: /device:TPU:1 before, /device:TPU:0 now
where the time goes in v5:
time: 19.3 us; the launch traced here: 19.1 us
  Pallas kernels  11.8 us (61%)
  starting transfers between devices  6.15 us (32%)
  local copies, waits for them, and re-layouts  0.65 us (3%)
  waiting for transfers between devices  0.41 us (2%)
    pallas_call x1, Pallas kernels, _local(): call(_refine, 'refine', [((2, TR, TC), f32)], [vmem] * 12, [hidden, pltpu...  7.47 us
    ppermute x4, starting transfers between devices, _exchange(): lax.ppermute(x, ('row', 'col'), _swaps(axis, k))  6.15 us
    pallas_call x1, Pallas kernels, _local(): call(_middle, 'middle', [((SEGS - 2,) + table, bf16), ((SEGS - 2,) + targ...  1.76 us
    pallas_call x1, Pallas kernels, _local(): call(_weights, 'weights', [((128, 48), bf16), ((384, 160), bf16), ((CH, 1...  1.62 us
    pallas_call x1, Pallas kernels, _local(): call(_pack_rows, 'pack_rows', [strip, strip, ((4 * TR, TC), f32)], [anywh...  0.83 us
    unnamed x2, local copies, waits for them, and re-layouts  0.65 us
    ppermute x4, waiting for transfers between devices, _exchange(): lax.ppermute(x, ('row', 'col'), _swaps(axis, k))  0.41 us
  transfers between devices with their start and end apart: 4, of which 1 were waited for; matrix products, arithmetic and copies ran while one was open for 0% of the time, Pallas kernels for 18%

profile of v5, /device:TPU:0, one launch (start us, length us, event | category | flops | bytes accessed | tf_op | source)
XLA Modules:
  0.0 19.1 jit_solution(11124843594196903724)
XLA Ops:
  0.0 0.8 %pack_rows.1 = (f32[48,128]{1,0:T(8,128)S(1)}, f32[48,128]{1,0:T(8,128)S(1)}, f32[128,128]{1,0:T(8,128)S(1)}) custom-call(bf16[32,128]{1,0:T(8,128)(2,1)} %mv_ref.1, bf16[32,128]{1,0:T(8,128)(2,1)} %fx_ref.1, f32[2,32,128]{2,1,0:T(8,128)} %fd_ref.1), custom_call_target="tpu_custom_call" | custom-call | tf_op jit(solution)/shard_map/pack_rows/pallas_call | solution.py:495
  0.8 0.5 %collective-permute-start = (f32[48,128]{1,0:T(8,128)S(1)}, f32[48,128]{1,0:T(8,128)S(1)}, u32[]{:S(2)}, u32[]{:S(2)}) collective-permute-start(f32[48,128]{1,0:T(8,128)S(1)} %get-tuple-element.18), channel_id=1, source_target_pairs={{0,1},{1,0},{2,3},{3,2},{4,5},{5,4},{6,7},{7,6},{8,16},{9,17},{10,... | collective-permute-start | bytes 73736 | tf_op jit(solution)/shard_map/ppermute | solution.py:474
  1.4 4.0 %collective-permute-start.1 = (f32[48,128]{1,0:T(8,128)S(1)}, f32[48,128]{1,0:T(8,128)S(1)}, u32[]{:S(2)}, u32[]{:S(2)}) collective-permute-start(f32[48,128]{1,0:T(8,128)S(1)} %get-tuple-element.19), channel_id=1, source_target_pairs={{0,8},{1,9},{2,10},{3,11},{4,12},{5,13},{6,14},{7,15},{8,0},{9,1},... | collective-permute-start | bytes 73736 | tf_op jit(solution)/shard_map/ppermute | solution.py:474
  5.3 0.0 copy-start
  5.3 0.7 %copy-done = f32[8]{0:T(128)S(1)} copy-done((f32[8]{0:T(128)S(1)}, f32[8]{0:T(128)}, u32[]{:S(2)}) %copy-start) | copy-done | bytes 56
  6.0 1.6 %weights.1 = (bf16[128,48]{1,0:T(8,128)(2,1)S(1)}, bf16[384,160]{1,0:T(8,128)(2,1)S(1)}, f32[8,128]{1,0:T(8,128)S(1)}) custom-call(f32[8,9]{1,0:T(8,128)} %w1_ref.1, f32[8,8,9]{2,1,0:T(8,128)} %w2_ref.1, f32[8]{0:T(128)S(1)} %copy-done), custom_call_target="tpu_custom_call" | custom-call | tf_op jit(solution)/shard_map/weights/pallas_call | solution.py:499
  7.6 0.0 collective-permute-done.down_ref
  7.6 0.0 collective-permute-done.1.up_ref
  7.6 0.1 pack_cols.1
  7.8 0.1 collective-permute-start.2
  7.8 1.6 %collective-permute-start.3 = (f32[24,128]{1,0:T(8,128)S(1)}, f32[24,128]{1,0:T(8,128)S(1)}, u32[]{:S(2)}, u32[]{:S(2)}) collective-permute-start(f32[24,128]{1,0:T(8,128)S(1)} %get-tuple-element.22), channel_id=1, source_target_pairs={{0,8},{1,2},{2,1},{3,4},{4,3},{5,6},{6,5},{7,15},{8,0},{9,10},{10,... | collective-permute-start | bytes 36872 | tf_op jit(solution)/shard_map/ppermute | solution.py:474
  9.4 1.8 %middle.1 = (bf16[3,1248,256]{2,1,0:T(8,128)(2,1)S(1)}, f32[3,10,8,128]{3,2,1,0:T(8,128)S(1)}, f32[2,10,8,128]{3,2,1,0:T(8,128)S(1)}, f32[2,72,8,128]{3,2,1,0:T(8,128)S(1)}) custom-call(f32[128,128]{1,0:T(8,128)S(1)} %get-tuple-element.17.own_ref, f32[48,128]{1,0:T(8,128)S(1)} %collective-permute-done.down_ref, f32[48,128]{1,0:T(8,128)S(1)} %collective-permute-done.1.up_ref, ...), custom_call_target="tpu_custom_call" | custom-call | tf_op jit(solution)/shard_map/middle/pallas_call | solution.py:507
  11.2 0.0 collective-permute-done.2.one_ref
  11.2 0.4 %collective-permute-done.3.two_ref = f32[24,128]{1,0:T(8,128)S(1)} collective-permute-done((f32[24,128]{1,0:T(8,128)S(1)}, f32[24,128]{1,0:T(8,128)S(1)}, u32[]{:S(2)}, u32[]{:S(2)}) %collective-permute-start.3) | collective-permute-done | bytes 12320 | tf_op jit(solution)/shard_map/ppermute | solution.py:474
  11.6 7.5 %refine.1 = f32[2,32,128]{2,1,0:T(8,128)} custom-call(f32[128,128]{1,0:T(8,128)S(1)} %get-tuple-element.17.own_ref, f32[48,128]{1,0:T(8,128)S(1)} %collective-permute-done.down_ref, f32[48,128]{1,0:T(8,128)S(1)} %collective-permute-done.1.up_ref, f32[24,128]{1,0:T(8,128)S(1)} %collective-permute-done.2.one_ref, ...), custom_call_target="tpu_custom_call" | custom-call | tf_op jit(solution)/shard_map/refine/pallas_call | solution.py:510
Async XLA Ops:
  0.8 6.8 %collective-permute-start = (f32[48,128]{1,0:T(8,128)S(1)}, f32[48,128]{1,0:T(8,128)S(1)}, u32[]{:S(2)}, u32[]{:S(2)}) collective-permute-start(f32[48,128]{1,0:T(8,128)S(1)} %get-tuple-element.18), channel_id=1, source_target_pairs={{0,1},{1,0},{2,3},{3,2},{4,5},{5,4},{6,7},{7,6},{8,16},{9,17},{10,... | collective-permute-start | bytes 73736 | tf_op jit(solution)/shard_map/ppermute | solution.py:474
  1.4 6.3 %collective-permute-start.1 = (f32[48,128]{1,0:T(8,128)S(1)}, f32[48,128]{1,0:T(8,128)S(1)}, u32[]{:S(2)}, u32[]{:S(2)}) collective-permute-start(f32[48,128]{1,0:T(8,128)S(1)} %get-tuple-element.19), channel_id=1, source_target_pairs={{0,8},{1,9},{2,10},{3,11},{4,12},{5,13},{6,14},{7,15},{8,0},{9,1},... | collective-permute-start | bytes 73736 | tf_op jit(solution)/shard_map/ppermute | solution.py:474
  5.3 0.7 %copy-start = (f32[8]{0:T(128)S(1)}, f32[8]{0:T(128)}, u32[]{:S(2)}) copy-start(f32[8]{0:T(128)} %bias_ref.1) | copy-start | bytes 100
  7.8 3.4 %collective-permute-start.2 = (f32[24,128]{1,0:T(8,128)S(1)}, f32[24,128]{1,0:T(8,128)S(1)}, u32[]{:S(2)}, u32[]{:S(2)}) collective-permute-start(f32[24,128]{1,0:T(8,128)S(1)} %get-tuple-element.21), channel_id=1, source_target_pairs={{0,1},{1,0},{2,3},{3,2},{4,5},{5,4},{6,7},{7,6},{8,9},{9,8},{10,11... | collective-permute-start | bytes 36872 | tf_op jit(solution)/shard_map/ppermute | solution.py:474
  7.8 3.8 %collective-permute-start.3 = (f32[24,128]{1,0:T(8,128)S(1)}, f32[24,128]{1,0:T(8,128)S(1)}, u32[]{:S(2)}, u32[]{:S(2)}) collective-permute-start(f32[24,128]{1,0:T(8,128)S(1)} %get-tuple-element.22), channel_id=1, source_target_pairs={{0,8},{1,2},{2,1},{3,4},{4,3},{5,6},{6,5},{7,15},{8,0},{9,10},{10,... | collective-permute-start | bytes 36872 | tf_op jit(solution)/shard_map/ppermute | solution.py:474

commit v6 on v5

--- a/solution.py
+++ b/solution.py
@@ -150,7 +150,7 @@
     m2_ref[...] = jnp.concatenate(hi_rows + lo_rows, axis=0)[:, :160].astype(jnp.bfloat16)
 
 
-def _pack_cols(own_ref, down_ref, up_ref, _, one_ref, two_ref):
+def _pack_cols(own_ref, up_ref, down_ref, _, one_ref, two_ref):
     even = lax.rem(lax.axis_index("col"), 2) == 0
     tall = _tall(_own(own_ref), up_ref[...], down_ref[...])
     lane = lax.broadcasted_iota(jnp.int32, (8, 128), 1)
@@ -279,7 +279,7 @@
                     jnp.where(mine & (sub // 4 == k), v, 0.0), axis=0, keepdims=True)
 
 
-def _middle(own_ref, down_ref, up_ref, w1_ref, bias_ref, w2_ref, e3_ref, ef_ref, raw_ref, rows_ref, hs):
+def _middle(own_ref, up_ref, down_ref, w1_ref, bias_ref, w2_ref, e3_ref, ef_ref, raw_ref, rows_ref, hs):
     moving, fixed, *field = _tall(_own(own_ref), up_ref[...], down_ref[...])
     lane = lax.broadcasted_iota(jnp.int32, (CH, 128), 1)
     rows = [{}, {}]
@@ -301,7 +301,7 @@
             pass
 
 
-def _refine(own_ref, down_ref, up_ref, one_ref, two_ref, w1_ref, bias_ref, w2_ref, mid3_ref, midf_ref, midr_ref, rows_ref,
+def _refine(own_ref, up_ref, down_ref, one_ref, two_ref, w1_ref, bias_ref, w2_ref, mid3_ref, midf_ref, midr_ref, rows_ref,
             out_ref, hs, e3, ef, raw, m1, m2, sq, disp, frac, idx, dat):
     place = _Place()
     row0, col0, rows, cols = place.row, place.col, place.rows, place.cols
@@ -501,16 +501,16 @@
         pltpu.VMEM((CH, 9), f32), pltpu.VMEM((CH, CH, 9), f32), pltpu.VMEM((2, CH, 128), f32),
         pltpu.SemaphoreType.DMA((2,))])(*[pltpu.with_memory_space_constraint(x, pltpu.HBM) for x in (first_weight, second_weight)], first_bias)
     strip = ((8 * pl.cdiv(TALL, 32), 128), f32)
-    one, two = _exchange(call(_pack_cols, "pack_cols", [strip, strip], [vmem] * 4, [])(own, down, up, bias), "col")
+    one, two = _exchange(call(_pack_cols, "pack_cols", [strip, strip], [vmem] * 4, [])(own, up, down, bias), "col")
     hidden = pltpu.VMEM((2, HROWS * CH, 256), bf16)
     table, target = (PROWS * 24, 256), (NQ, CH, 128)
     mid = call(_middle, "middle", [
         ((SEGS - 2,) + table, bf16), ((SEGS - 2,) + target, f32), ((2, NQ, 8, 128), f32), ((2, EROWS, CH, 128), f32),
-    ], [vmem] * 6, [hidden])(own, down, up, w1, bias, w2)
+    ], [vmem] * 6, [hidden])(own, up, down, w1, bias, w2)
     return call(_refine, "refine", [((2, TR, TC), f32)], [vmem] * 12, [
         hidden, pltpu.VMEM((2,) + table, bf16), pltpu.VMEM((2,) + target, f32),
         *[pltpu.VMEM((2, NQ, 8, 128), f32) for _ in range(8)],
-    ])(own, down, up, one, two, w1, bias, w2, *mid)[0]
+    ])(own, up, down, one, two, w1, bias, w2, *mid)[0]
 
 
 def solution(mesh):

time: 19.3 us -> 19.1 us (0.990)
  the two profiles are of different devices: /device:TPU:0 before, /device:TPU:5 now
where the time goes in v6:
time: 19.1 us; the launch traced here: 18.8 us
  Pallas kernels  11.8 us (62%)
  starting transfers between devices  4.73 us (25%)
  waiting for transfers between devices  1.61 us (8%)
  local copies, waits for them, and re-layouts  0.65 us (3%)
    pallas_call x1, Pallas kernels, _local(): call(_refine, 'refine', [((2, TR, TC), f32)], [vmem] * 12, [hidden, pltpu...  7.46 us
    ppermute x4, starting transfers between devices, _exchange(): lax.ppermute(x, ('row', 'col'), _swaps(axis, k))  4.73 us
    pallas_call x1, Pallas kernels, _local(): call(_middle, 'middle', [((SEGS - 2,) + table, bf16), ((SEGS - 2,) + targ...  1.76 us
    pallas_call x1, Pallas kernels, _local(): call(_weights, 'weights', [((128, 48), bf16), ((384, 160), bf16), ((CH, 1...  1.62 us
    ppermute x4, waiting for transfers between devices, _exchange(): lax.ppermute(x, ('row', 'col'), _swaps(axis, k))  1.61 us
    pallas_call x1, Pallas kernels, _local(): call(_pack_rows, 'pack_rows', [strip, strip, ((4 * TR, TC), f32)], [anywh...  0.83 us
    unnamed x2, local copies, waits for them, and re-layouts  0.65 us
  transfers between devices with their start and end apart: 4, of which 2 were waited for; matrix products, arithmetic and copies ran while one was open for 0% of the time, Pallas kernels for 18%

profile of v6, /device:TPU:5, one launch (start us, length us, event | category | flops | bytes accessed | tf_op | source)
XLA Modules:
  0.0 18.8 jit_solution(1066773009956890271)
XLA Ops:
  0.0 0.8 %pack_rows.1 = (f32[48,128]{1,0:T(8,128)S(1)}, f32[48,128]{1,0:T(8,128)S(1)}, f32[128,128]{1,0:T(8,128)S(1)}) custom-call(bf16[32,128]{1,0:T(8,128)(2,1)} %mv_ref.1, bf16[32,128]{1,0:T(8,128)(2,1)} %fx_ref.1, f32[2,32,128]{2,1,0:T(8,128)} %fd_ref.1), custom_call_target="tpu_custom_call" | custom-call | tf_op jit(solution)/shard_map/pack_rows/pallas_call | solution.py:495
  0.8 1.3 %collective-permute-start = (f32[48,128]{1,0:T(8,128)S(1)}, f32[48,128]{1,0:T(8,128)S(1)}, u32[]{:S(2)}, u32[]{:S(2)}) collective-permute-start(f32[48,128]{1,0:T(8,128)S(1)} %get-tuple-element.18), channel_id=1, source_target_pairs={{0,8},{1,9},{2,10},{3,11},{4,12},{5,13},{6,14},{7,15},{8,0},{9,1},... | collective-permute-start | bytes 73736 | tf_op jit(solution)/shard_map/ppermute | solution.py:474
  2.1 0.0 collective-permute-start.1
  2.1 0.0 copy-start
  2.1 0.7 %copy-done = f32[8]{0:T(128)S(1)} copy-done((f32[8]{0:T(128)S(1)}, f32[8]{0:T(128)}, u32[]{:S(2)}) %copy-start) | copy-done | bytes 56
  2.8 1.6 %weights.1 = (bf16[128,48]{1,0:T(8,128)(2,1)S(1)}, bf16[384,160]{1,0:T(8,128)(2,1)S(1)}, f32[8,128]{1,0:T(8,128)S(1)}) custom-call(f32[8,9]{1,0:T(8,128)} %w1_ref.1, f32[8,8,9]{2,1,0:T(8,128)} %w2_ref.1, f32[8]{0:T(128)S(1)} %copy-done), custom_call_target="tpu_custom_call" | custom-call | tf_op jit(solution)/shard_map/weights/pallas_call | solution.py:499
  4.4 0.0 collective-permute-done.up_ref
  4.4 1.3 %collective-permute-done.1.down_ref = f32[48,128]{1,0:T(8,128)S(1)} collective-permute-done((f32[48,128]{1,0:T(8,128)S(1)}, f32[48,128]{1,0:T(8,128)S(1)}, u32[]{:S(2)}, u32[]{:S(2)}) %collective-permute-start.1) | collective-permute-done | bytes 24608 | tf_op jit(solution)/shard_map/ppermute | solution.py:474
  5.7 0.1 pack_cols.1
  5.8 2.2 %collective-permute-start.2 = (f32[24,128]{1,0:T(8,128)S(1)}, f32[24,128]{1,0:T(8,128)S(1)}, u32[]{:S(2)}, u32[]{:S(2)}) collective-permute-start(f32[24,128]{1,0:T(8,128)S(1)} %get-tuple-element.21), channel_id=1, source_target_pairs={{0,1},{1,0},{2,3},{3,2},{4,5},{5,4},{6,7},{7,6},{8,9},{9,8},{10,11... | collective-permute-start | bytes 36872 | tf_op jit(solution)/shard_map/ppermute | solution.py:474
  8.0 1.3 %collective-permute-start.3 = (f32[24,128]{1,0:T(8,128)S(1)}, f32[24,128]{1,0:T(8,128)S(1)}, u32[]{:S(2)}, u32[]{:S(2)}) collective-permute-start(f32[24,128]{1,0:T(8,128)S(1)} %get-tuple-element.22), channel_id=1, source_target_pairs={{0,8},{1,2},{2,1},{3,4},{4,3},{5,6},{6,5},{7,15},{8,0},{9,10},{10,... | collective-permute-start | bytes 36872 | tf_op jit(solution)/shard_map/ppermute | solution.py:474
  9.2 1.8 %middle.1 = (bf16[3,1248,256]{2,1,0:T(8,128)(2,1)S(1)}, f32[3,10,8,128]{3,2,1,0:T(8,128)S(1)}, f32[2,10,8,128]{3,2,1,0:T(8,128)S(1)}, f32[2,72,8,128]{3,2,1,0:T(8,128)S(1)}) custom-call(f32[128,128]{1,0:T(8,128)S(1)} %get-tuple-element.17.own_ref, f32[48,128]{1,0:T(8,128)S(1)} %collective-permute-done.up_ref, f32[48,128]{1,0:T(8,128)S(1)} %collective-permute-done.1.down_ref, ...), custom_call_target="tpu_custom_call" | custom-call | tf_op jit(solution)/shard_map/middle/pallas_call | solution.py:507
  11.0 0.0 collective-permute-done.2.one_ref
  11.0 0.3 %collective-permute-done.3.two_ref = f32[24,128]{1,0:T(8,128)S(1)} collective-permute-done((f32[24,128]{1,0:T(8,128)S(1)}, f32[24,128]{1,0:T(8,128)S(1)}, u32[]{:S(2)}, u32[]{:S(2)}) %collective-permute-start.3) | collective-permute-done | bytes 12320 | tf_op jit(solution)/shard_map/ppermute | solution.py:474
  11.4 7.5 %refine.1 = f32[2,32,128]{2,1,0:T(8,128)} custom-call(f32[128,128]{1,0:T(8,128)S(1)} %get-tuple-element.17.own_ref, f32[48,128]{1,0:T(8,128)S(1)} %collective-permute-done.up_ref, f32[48,128]{1,0:T(8,128)S(1)} %collective-permute-done.1.down_ref, f32[24,128]{1,0:T(8,128)S(1)} %collective-permute-done.2.one_ref, ...), custom_call_target="tpu_custom_call" | custom-call | tf_op jit(solution)/shard_map/refine/pallas_call | solution.py:510
Async XLA Ops:
  0.8 3.6 %collective-permute-start = (f32[48,128]{1,0:T(8,128)S(1)}, f32[48,128]{1,0:T(8,128)S(1)}, u32[]{:S(2)}, u32[]{:S(2)}) collective-permute-start(f32[48,128]{1,0:T(8,128)S(1)} %get-tuple-element.18), channel_id=1, source_target_pairs={{0,8},{1,9},{2,10},{3,11},{4,12},{5,13},{6,14},{7,15},{8,0},{9,1},... | collective-permute-start | bytes 73736 | tf_op jit(solution)/shard_map/ppermute | solution.py:474
  2.1 3.6 %collective-permute-start.1 = (f32[48,128]{1,0:T(8,128)S(1)}, f32[48,128]{1,0:T(8,128)S(1)}, u32[]{:S(2)}, u32[]{:S(2)}) collective-permute-start(f32[48,128]{1,0:T(8,128)S(1)} %get-tuple-element.19), channel_id=1, source_target_pairs={{0,1},{1,0},{2,3},{3,2},{4,5},{5,4},{6,7},{7,6},{8,16},{9,17},{10,... | collective-permute-start | bytes 73736 | tf_op jit(solution)/shard_map/ppermute | solution.py:474
  2.1 0.7 %copy-start = (f32[8]{0:T(128)S(1)}, f32[8]{0:T(128)}, u32[]{:S(2)}) copy-start(f32[8]{0:T(128)} %bias_ref.1) | copy-start | bytes 100
  5.8 5.2 %collective-permute-start.2 = (f32[24,128]{1,0:T(8,128)S(1)}, f32[24,128]{1,0:T(8,128)S(1)}, u32[]{:S(2)}, u32[]{:S(2)}) collective-permute-start(f32[24,128]{1,0:T(8,128)S(1)} %get-tuple-element.21), channel_id=1, source_target_pairs={{0,1},{1,0},{2,3},{3,2},{4,5},{5,4},{6,7},{7,6},{8,9},{9,8},{10,11... | collective-permute-start | bytes 36872 | tf_op jit(solution)/shard_map/ppermute | solution.py:474
  8.0 3.4 %collective-permute-start.3 = (f32[24,128]{1,0:T(8,128)S(1)}, f32[24,128]{1,0:T(8,128)S(1)}, u32[]{:S(2)}, u32[]{:S(2)}) collective-permute-start(f32[24,128]{1,0:T(8,128)S(1)} %get-tuple-element.22), channel_id=1, source_target_pairs={{0,8},{1,2},{2,1},{3,4},{4,3},{5,6},{6,5},{7,15},{8,0},{9,10},{10,... | collective-permute-start | bytes 36872 | tf_op jit(solution)/shard_map/ppermute | solution.py:474
